TPU v7x, 32 devices: a whole 2x2x4 slice. The times are simulated.
32 devices in a mesh: lat: 16 (over z, x, core), lon: 2 (over y).
Axes of the slice: x: 2, y: 2, z: 4, core: 2. Of those that a mesh axis runs over, the one named last changes fastest.
Arguments:
- x_tiles: bfloat16 [2, 64, 77, 256], P('lon', 'lat'), may hold values from -6 to 6
- tile_pos: int32 [2, 64], P('lon', 'lat'), may hold values from 0 to 511, as said below
- valid_rows: int32 [2, 64], P('lon', 'lat'), may hold values from 1 to 16
- stem_w: bfloat16 [77, 200], replicated, may hold values from -0.625 to 0.625
- dw_kernel: float32 [200, 49], replicated, may hold values from -0.875 to 0.875
- norm_gain: float32 [200], replicated, may hold values from 0.1 to 1.9
- w_in: bfloat16 [200, 800], replicated, may hold values from -0.4375 to 0.4375
- w_out: bfloat16 [800, 200], replicated, may hold values from -0.21875 to 0.21875
- cotangent: bfloat16 [2, 64, 200, 256], P('lon', 'lat'), may hold values from -3072 to 3072
Outputs:
- out_tiles: bfloat16 [2, 64, 200, 256], P('lon', 'lat')
- grad_w_in: float32 [200, 800], replicated
- grad_w_out: float32 [800, 200], replicated
- grad_kernel: float32 [200, 49], replicated
- grad_gain: float32 [200], replicated
Inputs may be any that keep to these rules, and one draw needn't show every extreme that they name: `tile_pos`: in each sector the places are distinct; in the order of place, the r-th active tile of a sector is held by lat index r % 16. At most 2 tiles of one device lie in one band block of 32 tiles, and this is reached; some band block is fully active in every sector.
All inputs are finite; a program needn't handle non-finite values.
Results may differ from a plain program's by a relative error of at most 0.0075.
Values may be sent and summed in bfloat16 or wider, within the bound.
A program may use at most 128 MiB of HBM per device.

v0:
```python
import jax
import jax.numpy as jnp
from jax import lax
from jax.sharding import PartitionSpec as P

C = 200
CIN = 77
KW = 7
TS = 16
BH = 64
BW = 128
K_TILES = 32


def extended(block, sides, width, periodic):
    for axis, dim in sides:
        count = lax.axis_size(axis)
        forward = [(i, i + 1) for i in range(count - 1)]
        if periodic:
            forward.append((count - 1, 0))
        backward = [(target, source) for source, target in forward]
        low = lax.ppermute(
            lax.slice_in_dim(block, block.shape[dim] - width, None, axis=dim), axis, forward
        )
        high = lax.ppermute(lax.slice_in_dim(block, 0, width, axis=dim), axis, backward)
        block = jnp.concatenate([low, block, high], axis=dim)
    return block


def gelu_tanh(value):
    return jax.nn.gelu(value, approximate=True)


def tiles_to_block(tiles):
    chan = tiles.shape[1]
    shaped = tiles.reshape(BH // TS, BW // TS, chan, TS, TS)
    return shaped.transpose(2, 0, 3, 1, 4).reshape(chan, BH, BW)


def block_to_tiles(block):
    chan = block.shape[0]
    shaped = block.reshape(chan, BH // TS, TS, BW // TS, TS)
    return shaped.transpose(1, 3, 0, 2, 4).reshape(K_TILES, chan, TS * TS)


def select_rows(onehot, tiles):
    return jnp.einsum("qa,acp->qcp", onehot, tiles, preferred_element_type=jnp.float32).astype(
        jnp.bfloat16
    )


def body(x_tiles, tile_pos, valid_rows, stem_w, dw_kernel, norm_gain, w_in, w_out, cotangent):
    f32 = jnp.float32
    bf16 = jnp.bfloat16
    lat_count = lax.axis_size("lat")
    per_pair = (K_TILES + lat_count - 1) // lat_count
    slot_count = lat_count * per_pair
    cells = TS * TS
    inputs = x_tiles[0]
    places = tile_pos[0]
    ocean_rows = valid_rows[0]
    upstream = cotangent[0]
    tile_count = inputs.shape[0]
    cell_rows = jnp.arange(cells, dtype=jnp.int32) // TS
    ocean = cell_rows[None, :] < ocean_rows[:, None]
    masked_in = jnp.where(ocean[:, None, :], inputs, jnp.zeros_like(inputs))
    stem_tiles = jnp.einsum("kc,akp->acp", stem_w, masked_in, preferred_element_type=f32).astype(
        bf16
    )
    band_of = places // K_TILES
    local_place = places - band_of * K_TILES
    tile_order = jnp.arange(tile_count, dtype=jnp.int32)
    earlier = (band_of[None, :] == band_of[:, None]) & (tile_order[None, :] < tile_order[:, None])
    rank_in = jnp.sum(earlier.astype(jnp.int32), axis=1)
    slot_of = band_of * per_pair + rank_in
    route_map = jnp.arange(slot_count, dtype=jnp.int32)[:, None] == slot_of[None, :]
    route_b = route_map.astype(bf16)
    slot_place = jnp.sum(jnp.where(route_map, local_place[None, :] + 1, 0), axis=1) - 1
    slot_place = slot_place.reshape(lat_count, per_pair)
    outgoing = select_rows(route_b, masked_in).reshape(lat_count, per_pair, CIN, cells)
    arrived_raw, arrived_place = (
        lax.all_to_all(outgoing, "lat", split_axis=0, concat_axis=0, tiled=True),
        lax.all_to_all(slot_place, "lat", split_axis=0, concat_axis=0, tiled=True),
    )
    arrived_raw = arrived_raw.reshape(slot_count, CIN, cells)
    arrived = jnp.einsum("kc,akp->acp", stem_w, arrived_raw, preferred_element_type=f32).astype(
        bf16
    )
    placing = (
        jnp.arange(K_TILES, dtype=jnp.int32)[:, None] == arrived_place.reshape(slot_count)[None, :]
    )
    placing_b = placing.astype(bf16)
    band_field = tiles_to_block(select_rows(placing_b, arrived))
    reach = KW // 2
    widened = extended(band_field, (("lon", 2),), reach, True)
    padded = extended(widened, (("lat", 1),), reach, False)

    def window(tap_index):
        row_off = tap_index // KW
        col_off = tap_index % KW
        return padded[:, row_off : row_off + BH, col_off : col_off + BW].astype(f32)

    conv_out = jnp.zeros(band_field.shape, f32)
    for tap_index in range(KW * KW):
        conv_out = conv_out + dw_kernel[:, tap_index][:, None, None] * window(tap_index)
    centred = conv_out - jnp.mean(conv_out, axis=0, keepdims=True)
    inv_std = lax.rsqrt(jnp.mean(centred * centred, axis=0, keepdims=True) + 1e-06)
    unit = centred * inv_std
    normed = (unit * norm_gain[:, None, None]).astype(bf16)
    returning = select_rows(placing_b.T, block_to_tiles(normed)).reshape(
        lat_count, per_pair, C, cells
    )
    returned = lax.all_to_all(returning, "lat", split_axis=0, concat_axis=0, tiled=True).reshape(
        slot_count, C, cells
    )
    features = select_rows(route_b.T, returned)
    preact = jnp.einsum("ch,acp->ahp", w_in, features, preferred_element_type=f32)
    hidden = gelu_tanh(preact).astype(bf16)
    branch = jnp.einsum("hc,ahp->acp", w_out, hidden, preferred_element_type=f32)
    result = jnp.where(ocean[:, None, :], stem_tiles.astype(f32) + branch, 0.0).astype(bf16)
    masked_grad = jnp.where(ocean[:, None, :], upstream, jnp.zeros_like(upstream))
    grad_hidden = jnp.einsum("hc,acp->ahp", w_out, masked_grad, preferred_element_type=f32)
    grad_preact = jax.vjp(gelu_tanh, preact)[1](grad_hidden)[0].astype(bf16)
    grad_feats = jnp.einsum("ch,ahp->acp", w_in, grad_preact, preferred_element_type=f32).astype(
        bf16
    )
    grad_outgoing = select_rows(route_b, grad_feats).reshape(lat_count, per_pair, C, cells)
    grad_arrived = lax.all_to_all(
        grad_outgoing, "lat", split_axis=0, concat_axis=0, tiled=True
    ).reshape(slot_count, C, cells)
    sum_in = jnp.einsum("acp,ahp->ch", features, grad_preact, preferred_element_type=f32)
    sum_out = jnp.einsum("ahp,acp->hc", hidden, masked_grad, preferred_element_type=f32)
    grad_field = tiles_to_block(select_rows(placing_b, grad_arrived)).astype(f32)
    scaled = grad_field * norm_gain[:, None, None]
    grad_conv = inv_std * (
        scaled
        - jnp.mean(scaled, axis=0, keepdims=True)
        - unit * jnp.mean(scaled * unit, axis=0, keepdims=True)
    )
    kernel_terms = []
    for tap_index in range(KW * KW):
        kernel_terms.append(jnp.sum(grad_conv * window(tap_index), axis=(1, 2)))
    sum_kernel = jnp.stack(kernel_terms, axis=1)
    sum_gain = jnp.sum(grad_field * unit, axis=(1, 2))
    cell_sum = TS * jnp.sum(ocean_rows.astype(f32))
    total_in, total_out, total_kernel, total_gain, cell_total = lax.psum(
        (sum_in, sum_out, sum_kernel, sum_gain, cell_sum), ("lat", "lon")
    )
    return (
        result[None],
        total_in / cell_total,
        total_out / cell_total,
        total_kernel / cell_total,
        total_gain / cell_total,
    )


def solution(mesh):
    in_specs = (
        P("lon", "lat", None, None),
        P("lon", "lat"),
        P("lon", "lat"),
        P(),
        P(),
        P(),
        P(),
        P(),
        P("lon", "lat", None, None),
    )
    out_specs = (P("lon", "lat", None, None), P(), P(), P(), P())
    return jax.shard_map(body, mesh=mesh, in_specs=in_specs, out_specs=out_specs, check_vma=False)
```

profile of v0, /device:TPU:0, one launch (start us, length us, event | category | flops | bytes accessed | tf_op | source)
XLA Modules:
  0.0 635.8 jit_solution(10093161405181683781)
XLA Ops:
  7.2 0.7 and_select_fusion
  7.9 0.7 add_bitcast_fusion
  8.9 0.7 sub.49
  9.6 7.4 %all-to-all-start = ((s32[16,1,2]{2,1,0:T(1,128)}), s32[16,1,2]{2,1,0:T(1,128)S(1)}, u32[]{:S(2)}, u32[]{:S(2)}) async-start(s32[16,1,2]{2,1,0:T(1,128)} %bitcast.9), calls=%async_computation | async-start | bytes 16384 | tf_op jit(solution)/shard_map/all_to_all | solution.py:83
  16.9 0.7 broadcast_compare_fusion
  17.7 1.0 bitcast_select_fusion.3
  18.6 0.6 convolution_convert_fusion.2
  19.8 1.9 copy.69
  21.7 1.5 all-to-all-done
  23.3 4.5 all-to-all-start.1
  28.3 0.7 reduce.5
  29.0 25.2 %all-to-all-done.1 = bf16[16,2,77,256]{3,1,2,0:T(2,128)(2,1)S(1)} async-done(((bf16[16,2,77,256]{3,1,2,0:T(2,128)(2,1)}), bf16[16,2,77,256]{3,1,2,0:T(2,128)(2,1)S(1)}, u32[]{:S(2)}, u32[]{:S(2)}) %all-to-all-start.1) | async-done | bytes 1261600 | tf_op jit(solution)/shard_map/all_to_all | solution.py:82
  54.5 1.1 convert_bitcast_fusion
  55.6 2.7 fusion.114
  58.3 7.2 %copy.72 = bf16[32,200,256]{1,2,0:T(8,128)(2,1)} copy(bf16[32,200,256]{2,0,1:T(8,128)(2,1)} %fusion.114) | data formatting | bytes 6553600 | tf_op jit(solution)/shard_map/convert_element_type | solution.py:47
  65.5 2.8 copy.73
  68.4 1.6 collective-permute-start
  70.5 4.3 collective-permute-done
  74.9 2.6 collective-permute-done.1
  77.6 1.8 collective-permute-start.2
  79.4 1.5 collective-permute-start.3
  81.0 3.8 collective-permute-done.3
  84.7 8.1 %maximum_maximum_fusion = (bf16[200,67,134]{0,2,1:T(8,128)(2,1)S(1)}, bf16[200,67,134]{0,2,1:T(8,128)(2,1)S(1)}) fusion(bf16[200,64,3]{0,2,1:T(4,128)(2,1)S(1)} %collective-permute-done.1, bf16[200,64,128]{0,2,1:T(8,128)(2,1)S(1)} %bitcast.228, bf16[200,64,3]{0,2,1:T(4,128)(2,1)S(1)} %collective-permute-done, ...), kind=kLoop, calls=%fused_computation.208 | loop fusion | flops 28729600 | bytes 10934400 | tf_op jit(solution)/shard_map/concatenate | solution.py:26
  92.8 68.1 %fusion.152 = (f32[64,128]{1,0:T(8,128)S(1)}, f32[200,64,128]{0,2,1:T(8,128)S(1)}) fusion(bf16[200,67,134]{0,2,1:T(8,128)(2,1)S(1)} %get-tuple-element.77, f32[200]{0:T(256)S(1)} %bitcast.286, f32[200]{0:T(256)S(1)} %bitcast.287, f32[200]{0:T(256)S(1)} %bitcast.240, f32[200]{0:T(256)S(1)} %bitcast.241, f32[200]{0:T(256)S(1)} %bitcast.242, ...), kind=kLoop, calls=%fused_computation.307 | loop fusion | flops 270327808 | bytes 147681568 | tf_op jit(solution)/shard_map/reduce_sum | solution.py:106
  161.0 2.5 multiply_reduce_fusion.3
  163.5 2.6 multiply_convert_fusion
  166.1 2.6 copy.74
  168.7 7.3 %copy.76 = bf16[32,200,256]{2,0,1:T(8,128)(2,1)} copy(bf16[32,200,256]{1,2,0:T(8,128)(2,1)} %bitcast.237) | data formatting | bytes 6553600 | tf_op jit(solution)/shard_map/reshape | solution.py:43
  175.9 4.8 convolution_convert_fusion.1
  180.7 7.5 %reshape.217 = bf16[16,2,200,256]{3,1,0,2:T(2,128)(2,1)} reshape(bf16[32,200,256]{2,0,1:T(8,128)(2,1)} %convolution_convert_fusion.1) | data formatting | bytes 6553600 | tf_op jit(solution)/shard_map/reshape | solution.py:110
  188.3 4.2 copy.77
  192.4 84.9 %all_to_all.21 = bf16[16,2,200,256]{3,1,2,0:T(2,128)(2,1)S(1)} all-to-all(bf16[16,2,200,256]{3,1,2,0:T(2,128)(2,1)S(1)} %copy.77), channel_id=1, replica_groups=mesh['lat'=16,'lon'=2] {'lat'}, dimensions={0} | all-to-all | bytes 6553600 | tf_op jit(solution)/shard_map/all_to_all | solution.py:113
  277.3 5.5 copy.78
  282.9 7.8 %reshape.218 = bf16[32,200,256]{2,0,1:T(8,128)(2,1)} reshape(bf16[16,2,200,256]{3,1,0,2:T(2,128)(2,1)} %copy.78) | data formatting | bytes 6553600 | tf_op jit(solution)/shard_map/reshape | solution.py:113
  290.7 2.5 convolution_convert_fusion.4
  293.2 0.6 fusion.124
  293.9 3.7 fusion.107
  297.6 0.6 fusion.120
  298.2 2.8 convolution_convert_fusion
  301.0 7.6 %reshape.219 = bf16[16,2,200,256]{3,1,0,2:T(2,128)(2,1)} reshape(bf16[32,200,256]{2,0,1:T(8,128)(2,1)} %convolution_convert_fusion) | data formatting | bytes 6553600 | tf_op jit(solution)/shard_map/reshape | solution.py:127
  308.6 5.8 copy.82
  314.4 4.7 all-to-all-start.3
  319.2 0.6 convert_reduce_fusion.1
  320.4 1.2 fusion.119
  321.6 1.6 convolution_bitcast_fusion.1
  323.3 4.2 convolution_bitcast_fusion
  327.5 4.0 fusion.121
  331.6 55.5 %all-to-all-done.3 = bf16[16,2,200,256]{3,1,2,0:T(2,128)(2,1)} async-done(((bf16[16,2,200,256]{3,1,2,0:T(2,128)(2,1)}), bf16[16,2,200,256]{3,1,2,0:T(2,128)(2,1)}, u32[]{:S(2)}, u32[]{:S(2)}) %all-to-all-start.3) | async-done | bytes 3276832 | tf_op jit(solution)/shard_map/all_to_all | solution.py:128
  387.1 7.5 %copy.83 = bf16[16,2,200,256]{3,1,0,2:T(2,128)(2,1)} copy(bf16[16,2,200,256]{3,1,2,0:T(2,128)(2,1)} %all-to-all-done.3) | data formatting | bytes 6553600 | tf_op jit(solution)/shard_map/all_to_all | solution.py:128
  394.5 7.8 %reshape.220 = bf16[32,200,256]{2,0,1:T(8,128)(2,1)} reshape(bf16[16,2,200,256]{3,1,0,2:T(2,128)(2,1)} %copy.83) | data formatting | bytes 6553600 | tf_op jit(solution)/shard_map/reshape | solution.py:130
  402.3 5.6 convert_convert_fusion
  407.9 9.3 %copy.84 = f32[32,200,256]{1,2,0:T(8,128)} copy(f32[32,200,256]{2,0,1:T(8,128)} %convert_convert_fusion) | data formatting | bytes 13107200 | tf_op jit(solution)/shard_map/convert_element_type | solution.py:133
  417.3 4.6 multiply_reduce_fusion.2
  422.1 4.4 copy.85
  426.5 8.8 %multiply_reduce_fusion = (f32[200]{0:T(256)S(1)}, f32[64,128]{1,0:T(8,128)S(1)}) fusion(f32[200,64,128]{0,2,1:T(8,128)S(1)} %bitcast.231, f32[200,64,128]{0,2,1:T(8,128)} %copy-done.4, f32[64,128]{1,0:T(8,128)S(1)} %add_rsqrt_fusion, f32[64,128]{1,0:T(8,128)S(1)} %broadcast_multiply_fusion.1, f32[200]{0:T(256)S(1)} %copy-done.12), kind=kLoop, calls=%fused_computation.195 | loop fusion | flops 11460408 | bytes 13207104 | tf_op jit(solution)/shard_map/reduce_sum | solution.py:144
  435.3 50.6 %fusion.96 = (f32[200]{0:T(256)S(1)}, f32[200]{0:T(256)S(1)}, f32[200]{0:T(256)S(1)}, f32[200]{0:T(256)S(1)}, f32[200]{0:T(256)S(1)}, /*index=5*/f32[200]{0:T(25...) fusion(bf16[200,67,134]{0,2,1:T(8,128)(2,1)} %copy-done.3, ...), kind=kLoop, calls=%fused_computation.194 | loop fusion | flops 99938800 | bytes 78789472 | tf_op jit(solution)/shard_map/reduce_sum | solution.py:142
  485.9 49.7 %fusion.45 = (f32[200]{0:T(256)S(1)}, f32[200]{0:T(256)S(1)}, f32[200]{0:T(256)S(1)}, f32[200]{0:T(256)S(1)}, f32[200]{0:T(256)S(1)}, /*index=5*/f32[200]{0:T(25...) fusion(f32[200,64,128]{0,2,1:T(8,128)} %get-tuple-element.71, ...), kind=kLoop, calls=%fused_computation.143 | loop fusion | flops 88470000 | bytes 65550400 | tf_op jit(solution)/shard_map/reduce_sum | solution.py:142
  535.7 27.5 %fusion.78 = (f32[200]{0:T(256)S(1)}, f32[200]{0:T(256)S(1)}, f32[200]{0:T(256)S(1)}, f32[200]{0:T(256)S(1)}, f32[200]{0:T(256)S(1)}, /*index=5*/f32[200]{0:T(25...) fusion(f32[200,64,128]{0,2,1:T(8,128)} %get-tuple-element.71, ...), kind=kLoop, calls=%fused_computation.176 | loop fusion | flops 78641200 | bytes 19822400 | tf_op jit(solution)/shard_map/reduce_sum | solution.py:142
  563.3 4.3 fusion.27
  567.7 53.0 %all-reduce = (f32[]{:T(128)}, f32[200,49]{0,1:T(8,128)S(1)}, f32[200]{0:T(256)S(1)}) all-reduce(f32[]{:T(128)S(6)} %mul_shard_map.3, f32[200,49]{0,1:T(8,128)S(1)} %stack.199, f32[200]{0:T(256)S(1)} %get-tuple-element.5), channel_id=1, replica_groups=mesh['lat'=16,'lon'=2] {'lat','lon'}, use_global_device_ids=true, to_apply=%region_6.7 | all-reduce | flops 10001 | bytes 80008 | tf_op jit(solution)/shard_map/psum | solution.py:146
  620.8 2.7 broadcast_divide_fusion
  623.5 2.7 broadcast_divide_fusion.1
  626.2 1.3 broadcast_divide_fusion.2
  627.5 1.3 broadcast_divide_fusion.3
  (61 shorter events, 3.0 us)
Async XLA Ops:
  7.2 286.1 %copy-start = (bf16[200,800]{1,0:T(8,128)(2,1)S(1)}, bf16[200,800]{1,0:T(8,128)(2,1)}, u32[]{:S(2)}) copy-start(bf16[200,800]{1,0:T(8,128)(2,1)} %param.15) | copy-start | bytes 960004
  7.2 20.6 %copy-start.11 = (f32[200,49]{0,1:T(8,128)S(1)}, f32[200,49]{0,1:T(8,128)}, u32[]{:S(2)}) copy-start(f32[200,49]{0,1:T(8,128)} %param.13) | copy-start | bytes 117604
  7.2 47.3 %copy-start.10 = (bf16[77,200]{1,0:T(8,128)(2,1)S(1)}, bf16[77,200]{1,0:T(8,128)(2,1)}, u32[]{:S(2)}) copy-start(bf16[77,200]{1,0:T(8,128)(2,1)} %param.12) | copy-start | bytes 92404
  9.6 13.7 %all-to-all-start = ((s32[16,1,2]{2,1,0:T(1,128)}), s32[16,1,2]{2,1,0:T(1,128)S(1)}, u32[]{:S(2)}, u32[]{:S(2)}) async-start(s32[16,1,2]{2,1,0:T(1,128)} %bitcast.9), calls=%async_computation | async-start | bytes 16384 | tf_op jit(solution)/shard_map/all_to_all | solution.py:83
  23.3 31.0 %all-to-all-start.1 = ((bf16[16,2,77,256]{3,1,2,0:T(2,128)(2,1)}), bf16[16,2,77,256]{3,1,2,0:T(2,128)(2,1)S(1)}, u32[]{:S(2)}, u32[]{:S(2)}) async-start(bf16[16,2,77,256]{3,1,2,0:T(2,128)(2,1)} %copy.69), calls=%async_computation.1 | async-start | bytes 2523136 | tf_op jit(solution)/shard_map/all_to_all | solution.py:82
  68.3 24.5 %copy-start.6 = (bf16[200,4,16,8,16]{0,4,3,2,1:T(8,128)(2,1)}, bf16[200,4,16,8,16]{0,4,3,2,1:T(8,128)(2,1)S(1)}, u32[]{:S(2)}) copy-start(bf16[200,4,16,8,16]{0,4,3,2,1:T(8,128)(2,1)S(1)} %copy.73) | copy-start | bytes 9830404
  68.4 6.4 %collective-permute-start = (bf16[200,64,3]{0,2,1:T(4,128)(2,1)S(1)}, bf16[200,64,3]{0,2,1:T(4,128)(2,1)S(1)}, u32[]{:S(2)}, u32[]{:S(2)}) collective-permute-start(bf16[200,64,3]{0,2,1:T(4,128)(2,1)S(1)} %get-tuple-element.80), channel_id=1, source_target_pairs={{0,1},{1,0},{2,3},{3,2},{4,5},{5,4},{6,7},{7,6},{8,9},{9,8},{10,11... | collective-permute-start | bytes 230408 | tf_op jit(solution)/shard_map/ppermute | solution.py:22
  70.0 7.5 %collective-permute-start.1 = (bf16[200,64,3]{0,2,1:T(4,128)(2,1)S(1)}, bf16[200,64,3]{0,2,1:T(4,128)(2,1)S(1)}, u32[]{:S(2)}, u32[]{:S(2)}) collective-permute-start(bf16[200,64,3]{0,2,1:T(4,128)(2,1)S(1)} %get-tuple-element.81), channel_id=1, source_target_pairs={{1,0},{0,1},{3,2},{2,3},{5,4},{4,5},{7,6},{6,7},{9,8},{8,9},{11,10... | collective-permute-start | bytes 230408 | tf_op jit(solution)/shard_map/ppermute | solution.py:25
  77.6 3.3 collective-permute-start.2
  79.4 5.3 collective-permute-start.3
  92.8 68.1 %copy-start.2 = (bf16[200,67,134]{0,2,1:T(8,128)(2,1)}, bf16[200,67,134]{0,2,1:T(8,128)(2,1)S(1)}, u32[]{:S(2)}) copy-start(bf16[200,67,134]{0,2,1:T(8,128)(2,1)S(1)} %get-tuple-element.76) | copy-start | bytes 10773604
  92.8 68.1 %copy-start.3 = (bf16[200,67,134]{0,2,1:T(8,128)(2,1)}, bf16[200,67,134]{0,2,1:T(8,128)(2,1)S(1)}, u32[]{:S(2)}) copy-start(bf16[200,67,134]{0,2,1:T(8,128)(2,1)S(1)} %get-tuple-element.77) | copy-start | bytes 10773604
  161.0 5.1 copy-start.4
  161.0 2.5 copy-start.12
  282.8 11.0 %copy-start.14 = (bf16[800,200]{0,1:T(8,128)(2,1)S(1)}, bf16[800,200]{0,1:T(8,128)(2,1)}, u32[]{:S(2)}) copy-start(bf16[800,200]{0,1:T(8,128)(2,1)} %param.16) | copy-start | bytes 960004
  293.9 3.7 copy-start.8
  301.0 18.1 %copy-start.13 = (s32[1,4]{1,0:T(1,128)S(1)}, s32[1,4]{1,0:T(1,128)}, u32[]{:S(2)}) copy-start(s32[1,4]{1,0:T(1,128)} %param.11) | copy-start | bytes 52
  314.4 72.6 %all-to-all-start.3 = ((bf16[16,2,200,256]{3,1,2,0:T(2,128)(2,1)}), bf16[16,2,200,256]{3,1,2,0:T(2,128)(2,1)}, u32[]{:S(2)}, u32[]{:S(2)}) async-start(bf16[16,2,200,256]{3,1,2,0:T(2,128)(2,1)} %copy.82), calls=%async_computation.3 | async-start | bytes 6553600 | tf_op jit(solution)/shard_map/all_to_all | solution.py:128
  319.1 301.7 %all-reduce.4.cloned.1.call-start = ((), (), s32[]{:S(2)}) async-start(), calls=%async_computation.4 | async-start | bytes 2867200 | tf_op jit(solution)/shard_map/psum | solution.py:146
  323.3 4.3 copy-start.9
  426.5 8.8 %copy-start.7 = (f32[200,4,16,8,16]{0,4,3,2,1:T(8,128)}, f32[200,4,16,8,16]{0,4,3,2,1:T(8,128)S(1)}, u32[]{:S(2)}) copy-start(f32[200,4,16,8,16]{0,4,3,2,1:T(8,128)S(1)} %copy.85) | copy-start | bytes 19660804
  435.3 127.9 %slice-start = ((s8[4665344]{0:T(1024)(128)(4,1)}), s8[471040]{0:T(1024)(128)(4,1)S(1)}, s32[]{:S(2)}) async-start(s8[4665344]{0:T(1024)(128)(4,1)} %bitcast.224), calls=%async_computation.5 | async-start | bytes 942080
  485.9 77.3 %slice-start.1 = ((s8[4665344]{0:T(1024)(128)(4,1)}), s8[4194304]{0:T(1024)(128)(4,1)S(1)}, s32[]{:S(2)}) async-start(s8[4665344]{0:T(1024)(128)(4,1)} %bitcast.224), calls=%async_computation.6 | async-start | bytes 8388608
  535.7 27.6 %copy-start.5 = (f32[200,64,128]{0,2,1:T(8,128)S(1)}, f32[200,64,128]{0,2,1:T(8,128)}, u32[]{:S(2)}) copy-start(f32[200,64,128]{0,2,1:T(8,128)} %get-tuple-element.71) | copy-start | bytes 19660804
  535.7 93.1 %copy-start.1 = (bf16[200,800]{1,0:T(8,128)(2,1)S(1)}, bf16[200,800]{1,0:T(8,128)(2,1)}, u32[]{:S(2)}) copy-start(bf16[200,800]{1,0:T(8,128)(2,1)} %param.15) | copy-start | bytes 960004
Sparse Core Ops, SparseCore 0:
  327.6 169.5 all-reduce.3
where the time goes:
time: 643 us; the launch traced here: 636 us
  other arithmetic  240 us (37%)
  blocking collectives  138 us (21%)
  waiting for transfers between devices  93 us (14%)
  local copies, waits for them, and re-layouts  91.8 us (14%)
  matrix products  36.2 us (6%)
  starting transfers between devices  21.9 us (3%)
  between operations  15.4 us (2%)
    reduce_sum x4, other arithmetic, body(): kernel_terms.append(jnp.sum(grad_conv * window(tap_index), axis=(1, 2)))  132 us
    all_to_all x1, blocking collectives, body(): lax.all_to_all(returning, 'lat', split_axis=0, concat_axis=0, tiled=True)  84.9 us
    reduce_sum x1, other arithmetic, body(): centred = conv_out - jnp.mean(conv_out, axis=0, keepdims=True)  68.1 us
    all_to_all x1, waiting for transfers between devices, body(): lax.all_to_all(grad_outgoing, 'lat', split_axis=0, concat_axis=0, tiled=T...  55.5 us
    psum x1, blocking collectives, body(): lax.psum((sum_in, sum_out, sum_kernel, sum_gain, cell_sum), ('lat', 'lon'))  53 us
    all_to_all x1, waiting for transfers between devices, body(): lax.all_to_all(outgoing, 'lat', split_axis=0, concat_axis=0, tiled=True)  25.2 us
    dot_general x6, matrix products, select_rows(): jnp.einsum('qa,acp->qcp', onehot, tiles, preferred_element_type=jnp.float32)  19.1 us
    convert_element_type x2, local copies, waits for them, and re-layouts, body(): tiles_to_block(select_rows(placing_b, grad_arrived)).astype(f32)  13.7 us
  transfers between devices with their start and end apart: 8, of which 6 were waited for; matrix products, arithmetic and copies ran while one was open for 31% of the time, Pallas kernels for 0%

commit v1 on v0

v1 whole, which is shorter than its diff:
```python
import functools

import jax
import jax.numpy as jnp
import numpy as np
from jax import lax
from jax.experimental import pallas as pl
from jax.experimental.pallas import tpu as pltpu
from jax.sharding import PartitionSpec as P

TS = 16
CELLS = TS * TS
KW = 7
REACH = KW // 2
TCOLS = 8
EDGE = 160
PR = TS + 2 * REACH
PC = 24
CINP = 80
KROWS = CELLS + 8 * EDGE
OFFSETS = ((-1, -1), (-1, 0), (-1, 1), (0, -1), (0, 1), (1, -1), (1, 0), (1, 1))
VMEM_LIMIT = 56 * 1024 * 1024


def edge_index():
    table = -np.ones((TS, TS), np.int64)
    count = 0
    for y in range(TS):
        for x in range(TS):
            if min(y, x) < REACH or max(y, x) >= TS - REACH:
                table[y, x] = count
                count += 1
    return table


def edge_pick(tile_count):
    table = edge_index()
    pick = np.zeros((tile_count, CELLS, tile_count * EDGE), np.float32)
    for y in range(TS):
        for x in range(TS):
            if table[y, x] >= 0:
                for a in range(tile_count):
                    pick[a, y * TS + x, a * EDGE + table[y, x]] = 1
    return pick


def halo_pick():
    table = edge_index()
    pick = np.zeros((KROWS, PR * PC), np.float32)
    for py in range(PR):
        for px in range(PR):
            y, x = py - REACH, px - REACH
            dy, dx = y // TS, x // TS
            cell = py * PC + px
            if (dy, dx) == (0, 0):
                pick[y * TS + x, cell] = 1
            else:
                n = OFFSETS.index((dy, dx))
                pick[CELLS + n * EDGE + table[y % TS, x % TS], cell] = 1
    return pick


def pack_kernel(places, rows, x_ref, pick_ref, out_ref, held):
    tile_count = x_ref.shape[0]
    lanes = tile_count * EDGE
    cell_row = lax.broadcasted_iota(jnp.int32, (1, CELLS), 1) // TS
    total = jnp.zeros((x_ref.shape[1], lanes), jnp.float32)
    for a in range(tile_count):
        keep = (cell_row < rows[a]).astype(jnp.float32)
        tile = (x_ref[a].astype(jnp.float32) * keep).astype(jnp.bfloat16)
        total += jnp.dot(tile, pick_ref[a], preferred_element_type=jnp.float32)
    held[...] = jnp.zeros_like(held)
    held[0 : x_ref.shape[1], :] = total
    owner = lax.broadcasted_iota(jnp.int32, (1, lanes), 1) // EDGE
    high = jnp.zeros((1, lanes), jnp.int32)
    low = jnp.zeros((1, lanes), jnp.int32)
    ocean = jnp.zeros((1, lanes), jnp.int32)
    for a in range(tile_count):
        high = jnp.where(owner == a, places[a] // 16, high)
        low = jnp.where(owner == a, places[a] % 16, low)
        ocean = jnp.where(owner == a, rows[a], ocean)
    held[77:78, :] = high.astype(jnp.float32)
    held[78:79, :] = low.astype(jnp.float32)
    held[79:80, :] = ocean.astype(jnp.float32)
    out_ref[...] = held[...].astype(jnp.bfloat16)


def block_kernel(
    near, rows, gathered, x_ref, cot_ref, pick_ref, stem_ref, taps_ref, gain_ref, win_ref, wout_ref,
    out_ref, gin_ref, gout_ref, gker_ref, ggain_ref,
    sources, raw, padded, unit_s, inv_s, feats, hiddens, gpres, grads_t, gconv, kacc, gacc,
):
    f32 = jnp.float32
    bf16 = jnp.bfloat16
    tile_count, cin, _ = x_ref.shape
    chan = cot_ref.shape[1]
    lane_row = lax.broadcasted_iota(jnp.int32, (1, CELLS), 1) // TS
    kacc[...] = jnp.zeros_like(kacc)
    gacc[...] = jnp.zeros_like(gacc)
    sources[...] = jnp.zeros_like(sources)

    for a in range(tile_count):
        keep = (lane_row < rows[a]).astype(f32)
        tile = (x_ref[a].astype(f32) * keep).astype(bf16)
        sources[a, 0:cin, 0:CELLS] = tile
        for n in range(8):
            device = near[a, n, 0]
            slot = near[a, n, 1]
            block = gathered[device]
            piece = jnp.zeros((CINP, EDGE), bf16)
            for j in range(tile_count):
                piece = jnp.where(slot == j, block[:, j * EDGE : (j + 1) * EDGE], piece)
            sources[a, :, CELLS + n * EDGE : CELLS + (n + 1) * EDGE] = piece
    raw[...] = jnp.dot(
        sources[...].reshape(tile_count * CINP, KROWS), pick_ref[...], preferred_element_type=f32
    ).reshape(tile_count, CINP, PR * PC)

    @pl.loop(0, tile_count)
    def _(a):
        cells_in = raw[a].T.astype(bf16)
        stems = jnp.dot(cells_in, stem_ref[...], preferred_element_type=f32)
        padded[...] = stems.astype(bf16).astype(f32).reshape(PR, PC, chan)

        @pl.loop(0, TS // 4)
        def _(yb):
            y0 = yb * 4
            acc = jnp.zeros((4, TS, chan), f32)
            for k in range(KW):
                shifted = padded[pl.ds(y0, 4 + KW - 1), k : k + TS, :]
                for r in range(KW):
                    acc += taps_ref[r * KW + k : r * KW + k + 1, :][None] * shifted[r : r + 4]
            mean = jnp.mean(acc, axis=2, keepdims=True)
            centred = acc - mean
            inv = lax.rsqrt(jnp.mean(centred * centred, axis=2, keepdims=True) + 1e-06)
            unit_s[pl.ds(y0, 4)] = centred * inv
            inv_s[pl.ds(y0, 4)] = jnp.broadcast_to(inv, (4, TS, 128))

        gain = gain_ref[...]
        unit = unit_s[...].reshape(CELLS, chan)
        feat = (unit * gain).astype(bf16)
        feats[pl.ds(a * CELLS, CELLS), :] = feat
        pre = jnp.dot(feat, win_ref[...], preferred_element_type=f32)
        keep = (lane_row < rows[a]).astype(f32)
        mgrad_t = (cot_ref[a].astype(f32) * keep).astype(bf16)
        grads_t[a] = mgrad_t
        mgrad = mgrad_t.astype(f32).T.astype(bf16)
        ghid = lax.dot_general(mgrad, wout_ref[...], (((1,), (1,)), ((), ())), preferred_element_type=f32)
        square = pre * pre
        bend = jnp.tanh(0.7978845608028654 * pre * (1.0 + 0.044715 * square))
        half = 0.5 * (1.0 + bend)
        hidden = (pre * half).astype(bf16)
        slope = half + 0.5 * pre * (1.0 - bend * bend) * (0.7978845608028654 * (1.0 + 0.134145 * square))
        gpre = (ghid * slope).astype(bf16)
        hiddens[pl.ds(a * CELLS, CELLS), :] = hidden
        gpres[pl.ds(a * CELLS, CELLS), :] = gpre
        branch = jnp.dot(hidden, wout_ref[...], preferred_element_type=f32)
        stem_own = padded[REACH : REACH + TS, REACH : REACH + TS, :].reshape(CELLS, chan)
        out_ref[a] = ((stem_own + branch).T * keep).astype(bf16)
        gfeat = lax.dot_general(gpre, win_ref[...], (((1,), (1,)), ((), ())), preferred_element_type=f32)
        gfeat = gfeat.astype(bf16).astype(f32)
        gacc[...] += jnp.sum((gfeat * unit).reshape(CELLS // 8, 8, chan), axis=0)
        scaled = gfeat * gain
        first = jnp.mean(scaled, axis=1, keepdims=True)
        second = jnp.mean(scaled * unit, axis=1, keepdims=True)
        inv = inv_s[...].reshape(CELLS, 128)[:, 0:1]
        gconv[...] = (inv * (scaled - first - unit * second)).reshape(TS, TS, chan)

        @pl.loop(0, TS // 4)
        def _(yb):
            y0 = yb * 4
            grad = gconv[pl.ds(y0, 4)]
            for k in range(KW):
                shifted = padded[pl.ds(y0, 4 + KW - 1), k : k + TS, :]
                for r in range(KW):
                    prod = grad * shifted[r : r + 4]
                    kacc[r * KW + k] += jnp.sum(prod.reshape(8, 8, chan), axis=0)

    gin_ref[...] = lax.dot_general(
        feats[...], gpres[...], (((0,), (0,)), ((), ())), preferred_element_type=f32
    )
    total = jnp.zeros(gin_ref.shape, f32)
    for a in range(tile_count):
        total += jnp.dot(grads_t[a], hiddens[a * CELLS : (a + 1) * CELLS, :], preferred_element_type=f32)
    gout_ref[...] = total
    gker_ref[...] = jnp.sum(kacc[...], axis=1)
    ggain_ref[...] = jnp.sum(gacc[...], axis=0, keepdims=True)


def body(x_tiles, tile_pos, valid_rows, stem_w, dw_kernel, norm_gain, w_in, w_out, cotangent):
    f32 = jnp.float32
    bf16 = jnp.bfloat16
    lat_count = lax.axis_size("lat")
    lon_count = lax.axis_size("lon")
    inputs, places, rows, upstream = x_tiles[0], tile_pos[0], valid_rows[0], cotangent[0]
    tile_count, cin, _ = inputs.shape
    chan, hid = w_in.shape
    lanes = tile_count * EDGE
    smem = pl.BlockSpec(memory_space=pltpu.SMEM)
    vmem = pl.BlockSpec(memory_space=pltpu.VMEM)
    params = pltpu.CompilerParams(vmem_limit_bytes=VMEM_LIMIT)
    packed = pl.pallas_call(
        pack_kernel,
        out_shape=jax.ShapeDtypeStruct((CINP, lanes), bf16),
        in_specs=[smem, smem, vmem, vmem],
        out_specs=vmem,
        scratch_shapes=[pltpu.VMEM((CINP, lanes), f32)],
        compiler_params=params,
    )(places, rows, inputs, jnp.asarray(edge_pick(tile_count), bf16))
    gathered = lax.all_gather(packed, ("lon", "lat"))
    meta = gathered[:, 77:80, ::EDGE].astype(f32)
    all_place = (meta[:, 0, :] * 16.0 + meta[:, 1, :]).astype(jnp.int32)
    cell_total = TS * jnp.sum(meta[:, 2, :])
    count = lon_count * lat_count
    sector = jnp.arange(count, dtype=jnp.int32)[:, None] // lat_count
    row_all = all_place // TCOLS
    col_all = sector * TCOLS + all_place % TCOLS
    key_all = (row_all * (TCOLS * lon_count) + col_all).reshape(-1)
    off = np.array(OFFSETS, np.int32)
    my_row = places // TCOLS
    my_col = lax.axis_index("lon") * TCOLS + places % TCOLS
    want_row = my_row[:, None] + off[None, :, 0]
    want_col = (my_col[:, None] + off[None, :, 1]) % (TCOLS * lon_count)
    want = want_row * (TCOLS * lon_count) + want_col
    hit = want[:, :, None] == key_all[None, None, :]
    where = jnp.sum(jnp.where(hit, jnp.arange(count * tile_count, dtype=jnp.int32) + 1, 0), axis=2) - 1
    near = jnp.stack(
        [jnp.maximum(where, 0) // tile_count, jnp.where(where < 0, -1, where % tile_count)], axis=2
    )
    outs = pl.pallas_call(
        block_kernel,
        out_shape=[
            jax.ShapeDtypeStruct((tile_count, chan, CELLS), bf16),
            jax.ShapeDtypeStruct((chan, hid), f32),
            jax.ShapeDtypeStruct((chan, hid), f32),
            jax.ShapeDtypeStruct((KW * KW, chan), f32),
            jax.ShapeDtypeStruct((1, chan), f32),
        ],
        in_specs=[smem, smem] + [vmem] * 9,
        out_specs=[vmem] * 5,
        scratch_shapes=[
            pltpu.VMEM((tile_count, CINP, KROWS), bf16),
            pltpu.VMEM((tile_count, CINP, PR * PC), f32),
            pltpu.VMEM((PR, PC, chan), f32),
            pltpu.VMEM((TS, TS, chan), f32),
            pltpu.VMEM((TS, TS, 128), f32),
            pltpu.VMEM((tile_count * CELLS, chan), bf16),
            pltpu.VMEM((tile_count * CELLS, hid), bf16),
            pltpu.VMEM((tile_count * CELLS, hid), bf16),
            pltpu.VMEM((tile_count, chan, CELLS), bf16),
            pltpu.VMEM((TS, TS, chan), f32),
            pltpu.VMEM((KW * KW, 8, chan), f32),
            pltpu.VMEM((8, chan), f32),
        ],
        compiler_params=params,
    )(
        near, rows, gathered, inputs, upstream, jnp.asarray(halo_pick(), bf16),
        jnp.pad(stem_w, ((0, CINP - cin), (0, 0))), dw_kernel.T, norm_gain[None], w_in, w_out,
    )
    result, sum_in, sum_out, sum_kernel, sum_gain = outs
    sums = lax.psum((sum_in, sum_out, sum_kernel, sum_gain), ("lat", "lon"))
    scale = 1.0 / cell_total
    return (
        result[None],
        sums[0] * scale,
        sums[1].T * scale,
        sums[2].T * scale,
        sums[3][0] * scale,
    )


def solution(mesh):
    in_specs = (
        P("lon", "lat", None, None),
        P("lon", "lat"),
        P("lon", "lat"),
        P(),
        P(),
        P(),
        P(),
        P(),
        P("lon", "lat", None, None),
    )
    out_specs = (P("lon", "lat", None, None), P(), P(), P(), P())
    return jax.shard_map(body, mesh=mesh, in_specs=in_specs, out_specs=out_specs, check_vma=False)
```

time: 643 us -> 252 us (0.39); the launches traced: 636 us -> 252 us
  other arithmetic: 240 us -> 6.34 us
  blocking collectives: 138 us -> 39.5 us
  local copies, waits for them, and re-layouts: 91.8 us -> 5.39 us
  waiting for transfers between devices: 93 us -> 150 us
  matrix products: 36.2 us -> 0 us
  Pallas kernels: 0 us -> 35.8 us
  starting transfers between devices: 21.9 us -> 0.08 us
    reduce_sum x11 -> x2, other arithmetic: 217 us -> 0.91 us  [the longest x1 0.69 us: body(): cell_total = TS * jnp.sum(meta[:, 2, :])]
    psum x1, waiting for transfers between devices: 0.01 us -> 89.4 us  [body(): sums = lax.psum((sum_in, sum_out, sum_kernel, sum_gain), ('lat', 'lon'))]
    all_to_all x1 -> x0, blocking collectives: 84.9 us -> none  [body(): lax.all_to_all(returning, 'lat', split_axis=0, concat_axis=0, tiled=True)]
    all_to_all x3 -> x0, waiting for transfers between devices: 82.3 us -> none  [the longest x1 55.5 us: body(): lax.all_to_all(grad_outgoing, 'lat', split_axis=0, concat_axis=0, tiled=T...]
    all_gather x0 -> x1, waiting for transfers between devices: none -> 60.2 us  [body(): gathered = lax.all_gather(packed, ('lon', 'lat'))]
    reshape x9 -> x0, local copies, waits for them, and re-layouts: 50.4 us -> none  [the longest x2 13.4 us: body(): select_rows(route_b, grad_feats).reshape(lat_count, per_pair, C, cells)]
    dot_general x14 -> x0, matrix products: 36.2 us -> none  [the longest x6 19.1 us: select_rows(): jnp.einsum('qa,acp->qcp', onehot, tiles, preferred_element_type=jnp.float32)]
    pallas_call x0 -> x2, Pallas kernels: none -> 35.8 us  [the longest x1 33.4 us: body(): pl.pallas_call(block_kernel, out_shape=[jax.ShapeDtypeStruct((tile_count,...]
  transfers between devices with their start and end apart: 8 -> 2, of which waited for: 6 -> 2; matrix products, arithmetic and copies ran while one was open for 31% -> 1% of each run, Pallas kernels for 0% -> 0%
where the time goes in v1:
time: 252 us
  waiting for transfers between devices  150 us (60%)
  blocking collectives  39.5 us (16%)
  Pallas kernels  35.8 us (14%)
  between operations  14.8 us (6%)
  other arithmetic  6.34 us (3%)
  local copies, waits for them, and re-layouts  5.39 us (2%)
    psum x1, waiting for transfers between devices, body(): sums = lax.psum((sum_in, sum_out, sum_kernel, sum_gain), ('lat', 'lon'))  89.4 us
    all_gather x1, waiting for transfers between devices, body(): gathered = lax.all_gather(packed, ('lon', 'lat'))  60.2 us
    psum x1, blocking collectives, body(): sums = lax.psum((sum_in, sum_out, sum_kernel, sum_gain), ('lat', 'lon'))  39.5 us
    pallas_call x1, Pallas kernels, body(): pl.pallas_call(block_kernel, out_shape=[jax.ShapeDtypeStruct((tile_count,...  33.4 us
  transfers between devices with their start and end apart: 2, of which 2 were waited for; matrix products, arithmetic and copies ran while one was open for 1% of the time, Pallas kernels for 0%

profile of v1, /device:TPU:0, one launch (start us, length us, event | category | flops | bytes accessed | tf_op | source)
XLA Modules:
  0.0 251.5 jit_solution(8569141101693080758)
XLA Ops:
  7.2 0.0 copy-start.3
  7.2 0.0 copy-start.4
  7.2 0.0 copy-start.2
  7.2 0.0 copy-start
  7.2 0.0 copy-start.1
  7.2 0.0 all-gather.3.cloned.1.call-start
  7.3 1.6 copy.37
  8.9 2.4 shard_map.164
  11.3 0.0 all-gather.3.cloned.1.call-update
  11.3 0.0 all-reduce.5.cloned.1.call-start
  11.4 0.1 add.190
  11.5 0.1 add.191
  11.6 0.0 copy-done
  11.6 0.9 copy.35.wout_ref
  12.5 0.0 copy-done.1
  12.5 0.6 pad.4.stem_ref
  13.2 0.0 copy-done.2
  13.2 0.0 copy-done.3
  13.2 0.0 copy-done.4
  13.2 0.1 fusion.2
  13.3 60.2 %all-gather.3.cloned.1.call-done = bf16[2560,640]{1,0:T(8,128)(2,1)} async-done(((bf16[80,640]{1,0:T(8,128)(2,1)}), bf16[2560,640]{1,0:T(8,128)(2,1)}) %all-gather.3.cloned.1.call-update) | async-done | bytes 3276816 | tf_op jit(solution)/shard_map/all_gather | solution.py:209
  73.4 1.2 slice.12
  74.7 0.1 fusion.1
  74.7 0.1 convert_element_type.17
  74.9 0.2 select_reduce_fusion
  75.1 0.7 copy.34.near
  75.8 33.4 %shard_map.165 = (bf16[4,200,256]{2,1,0:T(8,128)(2,1)}, f32[200,800]{1,0:T(8,128)}, f32[200,800]{1,0:T(8,128)}, f32[49,200]{1,0:T(8,128)}, f32[1,200]{1,0:T(1,128)}) custom-call(s32[4,8,2]{2,1,0:T(8,128)} %copy.34.near, s32[4]{0:T(128)} %bitcast.36, bf16[32,80,640]{2,1,0:T(8,128)(2,1)} %bitcast.30, bf16[4,77,256]{2,1,0:T(8,128)(2,1)} %bitcast.32, ...), custom_call_target="tpu_custom_call" | custom-call | tf_op jit(solution)/shard_map/pallas_call | solution.py:229
  109.2 0.0 all-reduce.5.cloned.1.call-update
  109.2 0.7 slice_reduce_fusion
  110.6 39.5 %all-reduce.1 = (f32[49,200]{1,0:T(8,128)S(1)}, f32[1,200]{1,0:T(1,128)S(1)}) all-reduce(f32[49,200]{1,0:T(8,128)} %get-tuple-element.13, f32[1,200]{1,0:T(1,128)} %get-tuple-element.14), channel_id=1, replica_groups=mesh['lat'=16,'lon'=2] {'lat','lon'}, use_global_device_ids=true, to_apply=%region_4.5 | all-reduce | flops 10000 | bytes 80000 | tf_op jit(solution)/shard_map/psum | solution.py:260
  150.0 0.6 broadcast_multiply_fusion.1
  150.6 0.6 multiply_bitcast_fusion.1
  151.2 89.4 %all-reduce.5.cloned.1.call-done = (f32[200,800]{1,0:T(8,128)}, f32[200,800]{1,0:T(8,128)}) async-done(((f32[200,800]{1,0:T(8,128)}, f32[200,800]{1,0:T(8,128)}), (f32[200,800]{1,0:T(8,128)}, f32[200,800]{1,0:T(8,128)})) %all-reduce.5.cloned.1.call-update) | async-done | bytes 1280016 | tf_op jit(solution)/shard_map/psum | solution.py:260
  240.6 2.0 broadcast_multiply_fusion
  242.7 2.0 multiply_bitcast_fusion
  (6 shorter events, 0.1 us)
Async XLA Ops:
  7.2 6.0 %copy-start.3 = (s32[8]{0:T(128)S(1)}, s32[8]{0:T(128)}, u32[]{:S(2)}) copy-start(s32[8]{0:T(128)} %constant.135) | copy-start | bytes 100
  7.2 6.0 %copy-start.4 = (s32[8]{0:T(128)S(1)}, s32[8]{0:T(128)}, u32[]{:S(2)}) copy-start(s32[8]{0:T(128)} %constant.134) | copy-start | bytes 100
  7.2 6.0 %copy-start.2 = (s32[1,4]{1,0:T(1,128)S(1)}, s32[1,4]{1,0:T(1,128)}, u32[]{:S(2)}) copy-start(s32[1,4]{1,0:T(1,128)} %param.14) | copy-start | bytes 52
  7.2 4.4 %copy-start = (bf16[800,200]{0,1:T(8,128)(2,1)S(1)}, bf16[800,200]{0,1:T(8,128)(2,1)}, u32[]{:S(2)}) copy-start(bf16[800,200]{0,1:T(8,128)(2,1)} %param.20) | copy-start | bytes 960004
  7.2 5.3 %copy-start.1 = (bf16[77,200]{1,0:T(8,128)(2,1)S(1)}, bf16[77,200]{1,0:T(8,128)(2,1)}, u32[]{:S(2)}) copy-start(bf16[77,200]{1,0:T(8,128)(2,1)} %param.16) | copy-start | bytes 92404
  7.2 66.2 %all-gather.3.cloned.1.call-start = ((), (), s32[]{:S(2)}) async-start(), calls=%async_computation | async-start | bytes 3379200 | tf_op jit(solution)/shard_map/all_gather | solution.py:209
  11.3 229.3 %all-reduce.5.cloned.1.call-start = ((), (), s32[]{:S(2)}) async-start(), calls=%async_computation.1 | async-start | bytes 2867200 | tf_op jit(solution)/shard_map/psum | solution.py:260
Sparse Core Ops, SparseCore 0:
  11.5 61.9 all-gather.2
  109.3 131.2 all-reduce.4

commit v2 on v1

--- a/solution.py
+++ b/solution.py
@@ -19,6 +19,10 @@
 CINP = 80
 KROWS = CELLS + 8 * EDGE
 OFFSETS = ((-1, -1), (-1, 0), (-1, 1), (0, -1), (0, 1), (1, -1), (1, 0), (1, 1))
+SIDE = 896
+WIDE = 2 * SIDE
+ROWT = 13
+USED = ROWT * WIDE // 128
 VMEM_LIMIT = 56 * 1024 * 1024
 
 
@@ -87,8 +91,8 @@
 
 def block_kernel(
     near, rows, gathered, x_ref, cot_ref, pick_ref, stem_ref, taps_ref, gain_ref, win_ref, wout_ref,
-    out_ref, gin_ref, gout_ref, gker_ref, ggain_ref,
-    sources, raw, padded, unit_s, inv_s, feats, hiddens, gpres, grads_t, gconv, kacc, gacc,
+    out_ref, pack_ref,
+    held, small, sources, raw, padded, unit_s, inv_s, feats, hiddens, gpres, grads_t, gconv, kacc, gacc,
 ):
     f32 = jnp.float32
     bf16 = jnp.bfloat16
@@ -175,15 +179,172 @@
                     prod = grad * shifted[r : r + 4]
                     kacc[r * KW + k] += jnp.sum(prod.reshape(8, 8, chan), axis=0)
 
-    gin_ref[...] = lax.dot_general(
+    held[...] = jnp.zeros_like(held)
+    small[...] = jnp.zeros_like(small)
+    hid = win_ref.shape[1]
+    held[0:chan, 0:hid] = lax.dot_general(
         feats[...], gpres[...], (((0,), (0,)), ((), ())), preferred_element_type=f32
     )
-    total = jnp.zeros(gin_ref.shape, f32)
+    total = jnp.zeros((chan, hid), f32)
     for a in range(tile_count):
         total += jnp.dot(grads_t[a], hiddens[a * CELLS : (a + 1) * CELLS, :], preferred_element_type=f32)
-    gout_ref[...] = total
-    gker_ref[...] = jnp.sum(kacc[...], axis=1)
-    ggain_ref[...] = jnp.sum(gacc[...], axis=0, keepdims=True)
+    held[0:chan, SIDE : SIDE + hid] = total
+    small[0 : KW * KW, 0:chan] = jnp.sum(kacc[...], axis=1)
+    small[KW * KW : KW * KW + 1, 0:chan] = jnp.sum(gacc[...], axis=0, keepdims=True)
+    held[0:chan, hid:SIDE] = small[...].T[0:chan, 0 : SIDE - hid]
+    for t in range(WIDE // 128):
+        part = held[:, t * 128 : (t + 1) * 128].astype(bf16)
+        pack_ref[t * ROWT : (t + 1) * ROWT] = part.reshape(ROWT, 16, 128)
+    spare = pack_ref.shape[0] - USED
+    pack_ref[USED:] = jnp.zeros((spare, 16, 128), bf16)
+
+
+def unpack_kernel(total_ref, tiles_ref, gin_ref, gout_ref, gker_ref, ggain_ref, held):
+    scale = 1.0 / total_ref[0]
+    chan, hid = gin_ref.shape
+    for t in range(WIDE // 128):
+        part = tiles_ref[t * ROWT : (t + 1) * ROWT].astype(jnp.float32) * scale
+        held[:, t * 128 : (t + 1) * 128] = part.reshape(ROWT * 16, 128)
+    gin_ref[...] = held[0:chan, 0:hid]
+    gout_ref[...] = held[:, SIDE:WIDE].T[0:hid, 0:chan]
+    gker_ref[...] = held[0:chan, hid : hid + KW * KW]
+    base = SIDE - 128
+    flipped = held[:, base:SIDE].T
+    row = hid + KW * KW - base
+    ggain_ref[...] = flipped[row : row + 1, 0:chan]
+
+
+def greet(devices):
+    barrier = pltpu.get_barrier_semaphore()
+    for device in devices:
+        pl.semaphore_signal(barrier, inc=1, device_id=device, device_id_type=pl.DeviceIdType.MESH)
+    pl.semaphore_wait(barrier, len(devices))
+
+
+def gather_kernel(with_lon, src, out, send_sem, recv_sem, own_sem):
+    lat, lon = lax.axis_index("lat"), lax.axis_index("lon")
+    z, x, core = lat // 4, (lat // 2) % 2, lat % 2
+
+    def coords(step):
+        dz, dx, dy, dc = step
+        where = ((z + dz) % 4) * 4 + ((x + dx) % 2) * 2 + (core + dc) % 2
+        return where, (lon + dy) % 2 if with_lon else lon
+
+    def place(step):
+        where, sector = coords(step)
+        return sector * 16 + where if with_lon else where
+
+    def device_of(step):
+        where, sector = coords(step)
+        return {"lat": where, "lon": sector}
+
+    def number(step):
+        dz, dx, dy, dc = step
+        return ((dz * 2 + dx) * 2 + dy) * 2 + dc
+
+    peers = [(1, 0, 0, 0), (2, 0, 0, 0), (3, 0, 0, 0), (0, 1, 0, 0), (0, 0, 0, 1)]
+    if with_lon:
+        peers.append((0, 0, 1, 0))
+    greet([device_of(p) for p in peers])
+    copies = {}
+
+    def send(block, hop, landed):
+        here = src if block == (0, 0, 0, 0) else out.at[place(block)]
+        n = number(landed)
+        copy = pltpu.make_async_remote_copy(
+            src_ref=here, dst_ref=out.at[place(block)], send_sem=send_sem.at[n],
+            recv_sem=recv_sem.at[n], device_id=device_of(hop), device_id_type=pl.DeviceIdType.MESH,
+        )
+        copy.start()
+        copies[landed] = copy
+
+    def forward(block):
+        dz, dx, dy, dc = block
+        if dx == 0 and dy == 0:
+            send(block, (0, 1, 0, 0), (dz, 1, 0, 0))
+        if with_lon and dy == 0:
+            send(block, (0, 0, 1, 0), (dz, dx, 1, 0))
+        send(block, (0, 0, 0, 1), (dz, dx, dy, 1))
+
+    own = pltpu.make_async_copy(src, out.at[place((0, 0, 0, 0))], own_sem)
+    for dz in (1, 3, 2):
+        send((0, 0, 0, 0), (dz, 0, 0, 0), ((4 - dz) % 4, 0, 0, 0))
+    forward((0, 0, 0, 0))
+    own.start()
+    order = [(0, 1), (1, 0), (3, 0), (1, 1), (3, 1), (2, 0), (2, 1)]
+    blocks = [(dz, dx, 0, 0) for dz, dx in order]
+    if with_lon:
+        blocks += [(dz, dx, 1, 0) for dz, dx in [(0, 0)] + order]
+    for block in blocks:
+        copies[block].wait_recv()
+        forward(block)
+    for landed, copy in copies.items():
+        if landed[3] == 1:
+            copy.wait_recv()
+    for copy in copies.values():
+        copy.wait_send()
+    own.wait()
+
+
+def reduce_kernel(n_lon, per, src, out, first, acc, second, third, sems):
+    lat, lon = lax.axis_index("lat"), lax.axis_index("lon")
+    z = lat // 4
+    groups, deep = n_lon * 4, 4
+    span = per * deep
+    mine = lon * 4 + lat % 4
+
+    def in_plane(d):
+        g = (mine + d) % groups
+        return g, {"lat": z * 4 + g % 4, "lon": g // 4}
+
+    def along(d):
+        other = (z + d) % deep
+        return other, {"lat": other * 4 + lat % 4, "lon": lon}
+
+    greet([in_plane(d)[1] for d in range(1, groups)] + [along(d)[1] for d in range(1, deep)])
+    copies = []
+
+    def send(stage, back, here, there, device):
+        copy = pltpu.make_async_remote_copy(
+            src_ref=here, dst_ref=there, send_sem=sems.at[stage, 0, back], recv_sem=sems.at[stage, 1, back],
+            device_id=device, device_id_type=pl.DeviceIdType.MESH,
+        )
+        copy.start()
+        copies.append(copy)
+        return copy
+
+    landing = []
+    for d in range(1, groups):
+        g, device = in_plane(d)
+        landing.append(send(0, groups - d, src.at[pl.ds(g * span, span)], first.at[groups - d], device))
+    acc[...] = src[pl.ds(mine * span, span)].astype(jnp.float32)
+    for d in range(1, groups):
+        landing[d - 1].wait_recv()
+        acc[...] += first[groups - d].astype(jnp.float32)
+    second[...] = acc[...].astype(jnp.bfloat16)
+    landing = []
+    for d in range(1, deep):
+        other, device = along(d)
+        landing.append(send(1, deep - d, second.at[pl.ds(other * per, per)], third.at[deep - d], device))
+    total = acc[pl.ds(z * per, per)]
+    for d in range(1, deep):
+        landing[d - 1].wait_recv()
+        total += third[deep - d].astype(jnp.float32)
+    mark = pl.ds(mine * span + z * per, per)
+    out[mark] = total.astype(jnp.bfloat16)
+    landing = []
+    for d in range(1, deep):
+        landing.append(send(2, deep - d, out.at[mark], out.at[mark], along(d)[1]))
+    for copy in landing:
+        copy.wait_recv()
+    whole = pl.ds(mine * span, span)
+    landing = []
+    for d in range(1, groups):
+        landing.append(send(3, groups - d, out.at[whole], out.at[whole], in_plane(d)[1]))
+    for copy in landing:
+        copy.wait_recv()
+    for copy in copies:
+        copy.wait_send()
 
 
 def body(x_tiles, tile_pos, valid_rows, stem_w, dw_kernel, norm_gain, w_in, w_out, cotangent):
@@ -206,7 +367,24 @@
         scratch_shapes=[pltpu.VMEM((CINP, lanes), f32)],
         compiler_params=params,
     )(places, rows, inputs, jnp.asarray(edge_pick(tile_count), bf16))
-    gathered = lax.all_gather(packed, ("lon", "lat"))
+    with_lon = lon_count == 2
+    blocks = 32 if with_lon else 16
+    gathered = pl.pallas_call(
+        functools.partial(gather_kernel, with_lon),
+        out_shape=jax.ShapeDtypeStruct((blocks, CINP, lanes), bf16),
+        in_specs=[vmem],
+        out_specs=vmem,
+        scratch_shapes=[
+            pltpu.SemaphoreType.DMA((32,)),
+            pltpu.SemaphoreType.DMA((32,)),
+            pltpu.SemaphoreType.DMA,
+        ],
+        compiler_params=pltpu.CompilerParams(
+            vmem_limit_bytes=VMEM_LIMIT, collective_id=0, has_side_effects=True
+        ),
+    )(packed)
+    if not with_lon:
+        gathered = lax.all_gather(gathered, "lon", tiled=True)
     meta = gathered[:, 77:80, ::EDGE].astype(f32)
     all_place = (meta[:, 0, :] * 16.0 + meta[:, 1, :]).astype(jnp.int32)
     cell_total = TS * jnp.sum(meta[:, 2, :])
@@ -226,18 +404,20 @@
     near = jnp.stack(
         [jnp.maximum(where, 0) // tile_count, jnp.where(where < 0, -1, where % tile_count)], axis=2
     )
-    outs = pl.pallas_call(
+    groups = lon_count * 4
+    per = -(-USED // (groups * 4))
+    tiles_all = per * groups * 4
+    result, packed_sums = pl.pallas_call(
         block_kernel,
         out_shape=[
             jax.ShapeDtypeStruct((tile_count, chan, CELLS), bf16),
-            jax.ShapeDtypeStruct((chan, hid), f32),
-            jax.ShapeDtypeStruct((chan, hid), f32),
-            jax.ShapeDtypeStruct((KW * KW, chan), f32),
-            jax.ShapeDtypeStruct((1, chan), f32),
+            jax.ShapeDtypeStruct((tiles_all, 16, 128), bf16),
         ],
         in_specs=[smem, smem] + [vmem] * 9,
-        out_specs=[vmem] * 5,
+        out_specs=[vmem] * 2,
         scratch_shapes=[
+            pltpu.VMEM((ROWT * 16, WIDE), f32),
+            pltpu.VMEM((128, 256), f32),
             pltpu.VMEM((tile_count, CINP, KROWS), bf16),
             pltpu.VMEM((tile_count, CINP, PR * PC), f32),
             pltpu.VMEM((PR, PC, chan), f32),
@@ -256,16 +436,37 @@
         near, rows, gathered, inputs, upstream, jnp.asarray(halo_pick(), bf16),
         jnp.pad(stem_w, ((0, CINP - cin), (0, 0))), dw_kernel.T, norm_gain[None], w_in, w_out,
     )
-    result, sum_in, sum_out, sum_kernel, sum_gain = outs
-    sums = lax.psum((sum_in, sum_out, sum_kernel, sum_gain), ("lat", "lon"))
-    scale = 1.0 / cell_total
-    return (
-        result[None],
-        sums[0] * scale,
-        sums[1].T * scale,
-        sums[2].T * scale,
-        sums[3][0] * scale,
-    )
+    span = per * 4
+    reduced = pl.pallas_call(
+        functools.partial(reduce_kernel, lon_count, per),
+        out_shape=jax.ShapeDtypeStruct((tiles_all, 16, 128), bf16),
+        in_specs=[vmem],
+        out_specs=vmem,
+        scratch_shapes=[
+            pltpu.VMEM((groups, span, 16, 128), bf16),
+            pltpu.VMEM((span, 16, 128), f32),
+            pltpu.VMEM((span, 16, 128), bf16),
+            pltpu.VMEM((4, per, 16, 128), bf16),
+            pltpu.SemaphoreType.DMA((4, 2, groups)),
+        ],
+        compiler_params=pltpu.CompilerParams(
+            vmem_limit_bytes=VMEM_LIMIT, collective_id=1, has_side_effects=True
+        ),
+    )(packed_sums)
+    sum_in, sum_out, sum_kernel, sum_gain = pl.pallas_call(
+        unpack_kernel,
+        out_shape=[
+            jax.ShapeDtypeStruct((chan, hid), f32),
+            jax.ShapeDtypeStruct((hid, chan), f32),
+            jax.ShapeDtypeStruct((chan, KW * KW), f32),
+            jax.ShapeDtypeStruct((1, chan), f32),
+        ],
+        in_specs=[smem, vmem],
+        out_specs=[vmem] * 4,
+        scratch_shapes=[pltpu.VMEM((ROWT * 16, WIDE), f32)],
+        compiler_params=params,
+    )(cell_total.reshape(1), reduced)
+    return result[None], sum_in, sum_out, sum_kernel, sum_gain[0]
 
 
 def solution(mesh):

time: 252 us -> 115 us (0.46)
  waiting for transfers between devices: 150 us -> 0 us
  Pallas kernels: 35.8 us -> 99.9 us
  blocking collectives: 39.5 us -> 0 us
  between operations: 14.8 us -> 1.37 us
  local copies, waits for them, and re-layouts: 5.39 us -> 10 us
  other arithmetic: 6.34 us -> 2.43 us
    psum x1 -> x0, waiting for transfers between devices: 89.4 us -> none  [body(): sums = lax.psum((sum_in, sum_out, sum_kernel, sum_gain), ('lat', 'lon'))]
    pallas_call x0 -> x3, Pallas kernels: none -> 64 us  [the longest x1 31.6 us: body(): pl.pallas_call(functools.partial(reduce_kernel, lon_count, per), out_shap...]
    all_gather x1 -> x0, waiting for transfers between devices: 60.2 us -> none  [body(): gathered = lax.all_gather(packed, ('lon', 'lat'))]
    psum x1 -> x0, blocking collectives: 39.5 us -> none  [body(): sums = lax.psum((sum_in, sum_out, sum_kernel, sum_gain), ('lat', 'lon'))]
    mul x4 -> x0, other arithmetic: 5.22 us -> none  [the longest x1 2.01 us: body(): sums[0] * scale]
    unnamed x12 -> x6, local copies, waits for them, and re-layouts: 2.6 us -> 6.44 us
  transfers between devices with their start and end apart: 2 -> 0, of which waited for: 2 -> 0; matrix products, arithmetic and copies ran while one was open for 1% -> 0% of each run, Pallas kernels for 0% -> 0%
where the time goes in v2:
time: 115 us; the launch traced here: 114 us
  Pallas kernels  99.9 us (87%)
  local copies, waits for them, and re-layouts  10 us (9%)
  other arithmetic  2.43 us (2%)
  between operations  1.37 us (1%)
    pallas_call x1, Pallas kernels, body(): pl.pallas_call(block_kernel, out_shape=[jax.ShapeDtypeStruct((tile_count,...  33.4 us
    pallas_call x1, Pallas kernels, body(): pl.pallas_call(functools.partial(reduce_kernel, lon_count, per), out_shap...  31.6 us
    pallas_call x1, Pallas kernels, body(): pl.pallas_call(functools.partial(gather_kernel, with_lon), out_shape=jax....  30 us
    unnamed x6, local copies, waits for them, and re-layouts  6.44 us
    pallas_call x1, Pallas kernels, body(): pl.pallas_call(unpack_kernel, out_shape=[jax.ShapeDtypeStruct((chan, hid)...  2.44 us
    pallas_call x1, Pallas kernels, body(): pl.pallas_call(pack_kernel, out_shape=jax.ShapeDtypeStruct((CINP, lanes),...  2.41 us

profile of v2, /device:TPU:0, one launch (start us, length us, event | category | flops | bytes accessed | tf_op | source)
XLA Modules:
  0.0 113.7 jit_solution(18238369882560198094)
XLA Ops:
  0.6 0.0 copy-start
  0.7 0.7 and_select_fusion.4
  1.4 0.7 fusion.2
  2.1 0.1 add.182
  2.2 0.1 add.183
  2.3 1.4 %pad.4.stem_ref = bf16[80,200]{1,0:T(8,128)(2,1)} pad(bf16[77,200]{1,0:T(8,128)(2,1)} %param.16, bf16[]{:T(256)} %constant.120.clone.1), padding=0_3x0_0 | pad | bytes 62802 | tf_op jit(solution)/shard_map/jit(_pad)/pad | solution.py:437
  3.7 1.6 %copy.45 = bf16[1,4,77,256]{3,2,1,0:T(8,128)(2,1)} copy(bf16[1,4,77,256]{3,1,2,0:T(4,128)(2,1)} %param.13) | data formatting | bytes 315392 | tf_op args[0]
  5.3 2.4 %shard_map.164.src = bf16[80,640]{1,0:T(8,128)(2,1)} custom-call(s32[4]{0:T(128)} %bitcast.31, s32[4]{0:T(128)} %bitcast.29, bf16[4,77,256]{2,1,0:T(8,128)(2,1)} %bitcast.25, bf16[4,256,640]{2,1,0:T(8,128)(2,1)} %constant.122.clone.pick_ref), custom_call_target="tpu_custom_call" | custom-call | tf_op jit(solution)/shard_map/pallas_call | solution.py:362
  7.7 0.0 copy-done
  7.7 0.9 copy.41.wout_ref
  8.7 30.0 %shard_map.165.gathered = bf16[32,80,640]{2,1,0:T(8,128)(2,1)} custom-call(bf16[80,640]{1,0:T(8,128)(2,1)} %shard_map.164.src), custom_call_target="tpu_custom_call" | custom-call | tf_op jit(solution)/shard_map/pallas_call | solution.py:372
  38.7 1.2 %slice.12 = bf16[32,3,4]{2,1,0:T(4,128)(2,1)S(1)} slice(bf16[32,80,640]{2,1,0:T(8,128)(2,1)} %shard_map.165.gathered), slice={[0:32:1], [77:80:1], [0:640:160]} | slice | bytes 1536 | tf_op jit(solution)/shard_map/slice | solution.py:388
  39.9 0.6 slice_reduce_fusion
  41.2 0.1 fusion.1
  41.2 0.1 convert_element_type.17
  41.4 0.2 select_reduce_fusion
  41.6 0.7 copy.40.near
  42.3 33.4 %shard_map.166 = (bf16[4,200,256]{2,1,0:T(8,128)(2,1)}, bf16[192,16,128]{2,1,0:T(8,128)(2,1)}) custom-call(s32[4,8,2]{2,1,0:T(8,128)} %copy.40.near, s32[4]{0:T(128)} %bitcast.30, bf16[32,80,640]{2,1,0:T(8,128)(2,1)} %shard_map.165.gathered, bf16[4,77,256]{2,1,0:T(8,128)(2,1)} %bitcast.26, bf16[4,200,256]{2,1,0:T(8,128)(2,1)} %bitcast.27, ...), custom_call_target="tpu_custom_call" | custom-call | tf_op jit(solution)/shard_map/pallas_call | solution.py:410
  75.7 31.6 %shard_map.167.tiles_ref = bf16[192,16,128]{2,1,0:T(8,128)(2,1)} custom-call(bf16[192,16,128]{2,1,0:T(8,128)(2,1)} %get-tuple-element.12.src), custom_call_target="tpu_custom_call" | custom-call | tf_op jit(solution)/shard_map/pallas_call | solution.py:440
  107.3 2.4 %shard_map.168 = (f32[200,800]{1,0:T(8,128)}, f32[800,200]{1,0:T(8,128)}, f32[200,49]{1,0:T(8,128)}, f32[1,200]{1,0:T(1,128)}) custom-call(f32[1]{0:T(128)} %bitcast.8.total_ref, bf16[192,16,128]{2,1,0:T(8,128)(2,1)} %shard_map.167.tiles_ref), custom_call_target="tpu_custom_call" | custom-call | tf_op jit(solution)/shard_map/pallas_call | solution.py:456
  109.8 1.6 %copy.43 = f32[200,49]{0,1:T(8,128)} copy(f32[200,49]{1,0:T(8,128)} %get-tuple-element.35) | data formatting | bytes 78400
  111.4 2.3 %copy.42 = f32[800,200]{0,1:T(8,128)} copy(f32[800,200]{1,0:T(8,128)} %get-tuple-element.34) | data formatting | bytes 1280000
  (5 shorter events, 0.0 us)
Async XLA Ops:
  0.6 7.1 %copy-start = (bf16[800,200]{0,1:T(8,128)(2,1)S(1)}, bf16[800,200]{0,1:T(8,128)(2,1)}, u32[]{:S(2)}) copy-start(bf16[800,200]{0,1:T(8,128)(2,1)} %param.20) | copy-start | bytes 960004

commit v3 on v2

--- a/solution.py
+++ b/solution.py
@@ -17,12 +17,14 @@
 PR = TS + 2 * REACH
 PC = 24
 CINP = 80
-KROWS = CELLS + 8 * EDGE
+SIDE_CELLS = 64
+KEDGE = CELLS + 8 * EDGE
 OFFSETS = ((-1, -1), (-1, 0), (-1, 1), (0, -1), (0, 1), (1, -1), (1, 0), (1, 1))
 SIDE = 896
 WIDE = 2 * SIDE
 ROWT = 13
 USED = ROWT * WIDE // 128
+CROSS = tuple(n for n, (dy, dx) in enumerate(OFFSETS) if dx != 0)
 VMEM_LIMIT = 56 * 1024 * 1024
 
 
@@ -37,20 +39,28 @@
     return table
 
 
-def edge_pick(tile_count):
+def edge_pick():
     table = edge_index()
-    pick = np.zeros((tile_count, CELLS, tile_count * EDGE), np.float32)
+    pick = np.zeros((CELLS, EDGE), np.float32)
     for y in range(TS):
         for x in range(TS):
             if table[y, x] >= 0:
-                for a in range(tile_count):
-                    pick[a, y * TS + x, a * EDGE + table[y, x]] = 1
+                pick[y * TS + x, table[y, x]] = 1
     return pick
 
 
-def halo_pick():
+def side_pick():
+    pick = np.zeros((2, CELLS, SIDE_CELLS), np.float32)
+    for y in range(TS):
+        for x in range(REACH):
+            pick[0, y * TS + x, y * REACH + x] = 1
+            pick[1, y * TS + TS - REACH + x, y * REACH + x] = 1
+    return pick
+
+
+def halo_pick(with_lon):
     table = edge_index()
-    pick = np.zeros((KROWS, PR * PC), np.float32)
+    pick = np.zeros((KEDGE + 6 * SIDE_CELLS * with_lon, PR * PC), np.float32)
     for py in range(PR):
         for px in range(PR):
             y, x = py - REACH, px - REACH
@@ -61,38 +71,47 @@
             else:
                 n = OFFSETS.index((dy, dx))
                 pick[CELLS + n * EDGE + table[y % TS, x % TS], cell] = 1
+                if with_lon and dx != 0:
+                    part = (y % TS) * REACH + (x % TS if dx > 0 else x % TS - TS + REACH)
+                    pick[KEDGE + CROSS.index(n) * SIDE_CELLS + part, cell] = 1
     return pick
 
 
-def pack_kernel(places, rows, x_ref, pick_ref, out_ref, held):
-    tile_count = x_ref.shape[0]
-    lanes = tile_count * EDGE
+def pack_kernel(places, rows, x_ref, pick_ref, side_ref, out_ref, out_side_ref, held, held_side):
+    tile_count, cin, _ = x_ref.shape
     cell_row = lax.broadcasted_iota(jnp.int32, (1, CELLS), 1) // TS
-    total = jnp.zeros((x_ref.shape[1], lanes), jnp.float32)
+    held[...] = jnp.zeros_like(held)
+    held_side[...] = jnp.zeros_like(held_side)
     for a in range(tile_count):
         keep = (cell_row < rows[a]).astype(jnp.float32)
         tile = (x_ref[a].astype(jnp.float32) * keep).astype(jnp.bfloat16)
-        total += jnp.dot(tile, pick_ref[a], preferred_element_type=jnp.float32)
-    held[...] = jnp.zeros_like(held)
-    held[0 : x_ref.shape[1], :] = total
-    owner = lax.broadcasted_iota(jnp.int32, (1, lanes), 1) // EDGE
-    high = jnp.zeros((1, lanes), jnp.int32)
-    low = jnp.zeros((1, lanes), jnp.int32)
-    ocean = jnp.zeros((1, lanes), jnp.int32)
+        held[0:cin, a * EDGE : (a + 1) * EDGE] = jnp.dot(
+            tile, pick_ref[...], preferred_element_type=jnp.float32
+        )
+        outer = jnp.where((places[a] & (TCOLS - 1)) == 0, side_ref[0], side_ref[1])
+        held_side[0:cin, a * SIDE_CELLS : (a + 1) * SIDE_CELLS] = jnp.dot(
+            tile, outer, preferred_element_type=jnp.float32
+        )
+    owner = lax.broadcasted_iota(jnp.int32, (1, 128), 1)
+    high = jnp.zeros((1, 128), jnp.int32)
+    low = jnp.zeros((1, 128), jnp.int32)
+    ocean = jnp.zeros((1, 128), jnp.int32)
     for a in range(tile_count):
-        high = jnp.where(owner == a, places[a] // 16, high)
-        low = jnp.where(owner == a, places[a] % 16, low)
+        high = jnp.where(owner == a, places[a] >> 4, high)
+        low = jnp.where(owner == a, places[a] & 15, low)
         ocean = jnp.where(owner == a, rows[a], ocean)
-    held[77:78, :] = high.astype(jnp.float32)
-    held[78:79, :] = low.astype(jnp.float32)
-    held[79:80, :] = ocean.astype(jnp.float32)
+    for target in (held, held_side):
+        target[77:78, 0:128] = high.astype(jnp.float32)
+        target[78:79, 0:128] = low.astype(jnp.float32)
+        target[79:80, 0:128] = ocean.astype(jnp.float32)
     out_ref[...] = held[...].astype(jnp.bfloat16)
+    out_side_ref[...] = held_side[...].astype(jnp.bfloat16)
 
 
 def block_kernel(
-    near, rows, gathered, x_ref, cot_ref, pick_ref, stem_ref, taps_ref, gain_ref, win_ref, wout_ref,
+    with_lon, near, rows, gathered, sides, x_ref, cot_ref, pick_ref, stem_ref, taps_ref, gain_ref, win_ref, wout_ref,
     out_ref, pack_ref,
-    held, small, sources, raw, padded, unit_s, inv_s, feats, hiddens, gpres, grads_t, gconv, kacc, gacc,
+    held, small, stem_s, sources, raw, padded, unit_s, inv_s, feats, hiddens, gpres, grads_t, gconv, kacc, gacc,
 ):
     f32 = jnp.float32
     bf16 = jnp.bfloat16
@@ -102,27 +121,38 @@
     kacc[...] = jnp.zeros_like(kacc)
     gacc[...] = jnp.zeros_like(gacc)
     sources[...] = jnp.zeros_like(sources)
+    stem_s[...] = jnp.zeros_like(stem_s)
+    stem_s[0:cin, :] = stem_ref[...]
 
     for a in range(tile_count):
         keep = (lane_row < rows[a]).astype(f32)
         tile = (x_ref[a].astype(f32) * keep).astype(bf16)
         sources[a, 0:cin, 0:CELLS] = tile
         for n in range(8):
-            device = near[a, n, 0]
-            slot = near[a, n, 1]
-            block = gathered[device]
+            code = near[a, n]
+            slot = code & 7
+            block = gathered[code >> 3]
             piece = jnp.zeros((CINP, EDGE), bf16)
             for j in range(tile_count):
                 piece = jnp.where(slot == j, block[:, j * EDGE : (j + 1) * EDGE], piece)
             sources[a, :, CELLS + n * EDGE : CELLS + (n + 1) * EDGE] = piece
+        for m, n in enumerate(CROSS if with_lon else ()):
+            code = near[a, 8 + n]
+            slot = code & 7
+            block = sides[code >> 3]
+            piece = jnp.zeros((CINP, SIDE_CELLS), bf16)
+            for j in range(tile_count):
+                piece = jnp.where(slot == j, block[:, j * SIDE_CELLS : (j + 1) * SIDE_CELLS], piece)
+            start = KEDGE + m * SIDE_CELLS
+            sources[a, :, start : start + SIDE_CELLS] = piece
     raw[...] = jnp.dot(
-        sources[...].reshape(tile_count * CINP, KROWS), pick_ref[...], preferred_element_type=f32
+        sources[...].reshape(tile_count * CINP, pick_ref.shape[0]), pick_ref[...], preferred_element_type=f32
     ).reshape(tile_count, CINP, PR * PC)
 
     @pl.loop(0, tile_count)
     def _(a):
         cells_in = raw[a].T.astype(bf16)
-        stems = jnp.dot(cells_in, stem_ref[...], preferred_element_type=f32)
+        stems = jnp.dot(cells_in, stem_s[...], preferred_element_type=f32)
         padded[...] = stems.astype(bf16).astype(f32).reshape(PR, PC, chan)
 
         @pl.loop(0, TS // 4)
@@ -148,7 +178,7 @@
         mgrad_t = (cot_ref[a].astype(f32) * keep).astype(bf16)
         grads_t[a] = mgrad_t
         mgrad = mgrad_t.astype(f32).T.astype(bf16)
-        ghid = lax.dot_general(mgrad, wout_ref[...], (((1,), (1,)), ((), ())), preferred_element_type=f32)
+        ghid = jnp.dot(mgrad, wout_ref[...], preferred_element_type=f32)
         square = pre * pre
         bend = jnp.tanh(0.7978845608028654 * pre * (1.0 + 0.044715 * square))
         half = 0.5 * (1.0 + bend)
@@ -157,7 +187,9 @@
         gpre = (ghid * slope).astype(bf16)
         hiddens[pl.ds(a * CELLS, CELLS), :] = hidden
         gpres[pl.ds(a * CELLS, CELLS), :] = gpre
-        branch = jnp.dot(hidden, wout_ref[...], preferred_element_type=f32)
+        branch = lax.dot_general(
+            hidden, wout_ref[...], (((1,), (1,)), ((), ())), preferred_element_type=f32
+        )
         stem_own = padded[REACH : REACH + TS, REACH : REACH + TS, :].reshape(CELLS, chan)
         out_ref[a] = ((stem_own + branch).T * keep).astype(bf16)
         gfeat = lax.dot_general(gpre, win_ref[...], (((1,), (1,)), ((), ())), preferred_element_type=f32)
@@ -206,11 +238,11 @@
         part = tiles_ref[t * ROWT : (t + 1) * ROWT].astype(jnp.float32) * scale
         held[:, t * 128 : (t + 1) * 128] = part.reshape(ROWT * 16, 128)
     gin_ref[...] = held[0:chan, 0:hid]
-    gout_ref[...] = held[:, SIDE:WIDE].T[0:hid, 0:chan]
-    gker_ref[...] = held[0:chan, hid : hid + KW * KW]
+    gout_ref[...] = held[0:chan, SIDE : SIDE + hid]
     base = SIDE - 128
     flipped = held[:, base:SIDE].T
     row = hid + KW * KW - base
+    gker_ref[...] = flipped[hid - base : row, 0:chan]
     ggain_ref[...] = flipped[row : row + 1, 0:chan]
 
 
@@ -221,66 +253,67 @@
     pl.semaphore_wait(barrier, len(devices))
 
 
-def gather_kernel(with_lon, src, out, send_sem, recv_sem, own_sem):
+def gather_kernel(with_lon, src, side, out, out_side, send_sem, recv_sem, own_sem):
     lat, lon = lax.axis_index("lat"), lax.axis_index("lon")
     z, x, core = lat // 4, (lat // 2) % 2, lat % 2
 
-    def coords(step):
-        dz, dx, dy, dc = step
-        where = ((z + dz) % 4) * 4 + ((x + dx) % 2) * 2 + (core + dc) % 2
-        return where, (lon + dy) % 2 if with_lon else lon
-
     def place(step):
-        where, sector = coords(step)
-        return sector * 16 + where if with_lon else where
+        dz, dx, dc = step
+        return ((z + dz) % 4) * 4 + ((x + dx) % 2) * 2 + (core + dc) % 2
 
     def device_of(step):
-        where, sector = coords(step)
-        return {"lat": where, "lon": sector}
-
-    def number(step):
-        dz, dx, dy, dc = step
-        return ((dz * 2 + dx) * 2 + dy) * 2 + dc
-
-    peers = [(1, 0, 0, 0), (2, 0, 0, 0), (3, 0, 0, 0), (0, 1, 0, 0), (0, 0, 0, 1)]
-    if with_lon:
-        peers.append((0, 0, 1, 0))
-    greet([device_of(p) for p in peers])
+        return {"lat": place(step), "lon": lon}
+
+    across = {"lat": lat, "lon": (lon + 1) % 2}
+    peers = [device_of(p) for p in ((1, 0, 0), (2, 0, 0), (3, 0, 0), (0, 1, 0), (0, 0, 1))]
+    greet(peers + [across] * with_lon)
     copies = {}
 
-    def send(block, hop, landed):
-        here = src if block == (0, 0, 0, 0) else out.at[place(block)]
-        n = number(landed)
+    def start(key, here, there, n, device):
         copy = pltpu.make_async_remote_copy(
-            src_ref=here, dst_ref=out.at[place(block)], send_sem=send_sem.at[n],
-            recv_sem=recv_sem.at[n], device_id=device_of(hop), device_id_type=pl.DeviceIdType.MESH,
+            src_ref=here, dst_ref=there, send_sem=send_sem.at[n], recv_sem=recv_sem.at[n],
+            device_id=device, device_id_type=pl.DeviceIdType.MESH,
         )
         copy.start()
-        copies[landed] = copy
-
-    def forward(block):
-        dz, dx, dy, dc = block
-        if dx == 0 and dy == 0:
-            send(block, (0, 1, 0, 0), (dz, 1, 0, 0))
-        if with_lon and dy == 0:
-            send(block, (0, 0, 1, 0), (dz, dx, 1, 0))
-        send(block, (0, 0, 0, 1), (dz, dx, dy, 1))
-
-    own = pltpu.make_async_copy(src, out.at[place((0, 0, 0, 0))], own_sem)
-    for dz in (1, 3, 2):
-        send((0, 0, 0, 0), (dz, 0, 0, 0), ((4 - dz) % 4, 0, 0, 0))
-    forward((0, 0, 0, 0))
+        copies[key] = copy
+
+    def send(which, block, hop, landed):
+        target = out_side if which else out
+        here = target.at[place(block)]
+        if which == 0 and block == (0, 0, 0):
+            here = src
+        dz, dx, dc = landed
+        n = which * 16 + (dz * 2 + dx) * 2 + dc
+        start((which, landed), here, target.at[place(block)], n, device_of(hop))
+
+    def forward(which, block):
+        dz, dx, dc = block
+        if dx == 0:
+            send(which, block, (0, 1, 0), (dz, 1, 0))
+        send(which, block, (0, 0, 1), (dz, dx, 1))
+
+    def spread(which):
+        for dz in (2, 1, 3):
+            send(which, (0, 0, 0), (dz, 0, 0), ((4 - dz) % 4, 0, 0))
+        forward(which, (0, 0, 0))
+
+    if with_lon:
+        start("side", side, out_side.at[lat], 32, across)
+    spread(0)
+    own = pltpu.make_async_copy(src, out.at[lat], own_sem)
     own.start()
-    order = [(0, 1), (1, 0), (3, 0), (1, 1), (3, 1), (2, 0), (2, 1)]
-    blocks = [(dz, dx, 0, 0) for dz, dx in order]
     if with_lon:
-        blocks += [(dz, dx, 1, 0) for dz, dx in [(0, 0)] + order]
-    for block in blocks:
-        copies[block].wait_recv()
-        forward(block)
-    for landed, copy in copies.items():
-        if landed[3] == 1:
-            copy.wait_recv()
+        copies["side"].wait_recv()
+        spread(1)
+    kinds = (0, 1) if with_lon else (0,)
+    for dz, dx in ((0, 1), (1, 0), (3, 0), (1, 1), (3, 1), (2, 0), (2, 1)):
+        for which in kinds:
+            copies[which, (dz, dx, 0)].wait_recv()
+            forward(which, (dz, dx, 0))
+    for which in kinds:
+        for dz in range(4):
+            for dx in range(2):
+                copies[which, (dz, dx, 1)].wait_recv()
     for copy in copies.values():
         copy.wait_send()
     own.wait()
@@ -359,66 +392,89 @@
     smem = pl.BlockSpec(memory_space=pltpu.SMEM)
     vmem = pl.BlockSpec(memory_space=pltpu.VMEM)
     params = pltpu.CompilerParams(vmem_limit_bytes=VMEM_LIMIT)
-    packed = pl.pallas_call(
+    side_lanes = tile_count * SIDE_CELLS
+    packed, packed_side = pl.pallas_call(
         pack_kernel,
-        out_shape=jax.ShapeDtypeStruct((CINP, lanes), bf16),
-        in_specs=[smem, smem, vmem, vmem],
-        out_specs=vmem,
-        scratch_shapes=[pltpu.VMEM((CINP, lanes), f32)],
+        out_shape=[
+            jax.ShapeDtypeStruct((CINP, lanes), bf16),
+            jax.ShapeDtypeStruct((CINP, side_lanes), bf16),
+        ],
+        in_specs=[smem, smem, vmem, vmem, vmem],
+        out_specs=[vmem, vmem],
+        scratch_shapes=[pltpu.VMEM((CINP, lanes), f32), pltpu.VMEM((CINP, side_lanes), f32)],
         compiler_params=params,
-    )(places, rows, inputs, jnp.asarray(edge_pick(tile_count), bf16))
+    )(places, rows, inputs, jnp.asarray(edge_pick(), bf16), jnp.asarray(side_pick(), bf16))
     with_lon = lon_count == 2
-    blocks = 32 if with_lon else 16
-    gathered = pl.pallas_call(
+    gathered, sides = pl.pallas_call(
         functools.partial(gather_kernel, with_lon),
-        out_shape=jax.ShapeDtypeStruct((blocks, CINP, lanes), bf16),
-        in_specs=[vmem],
-        out_specs=vmem,
+        out_shape=[
+            jax.ShapeDtypeStruct((lat_count, CINP, lanes), bf16),
+            jax.ShapeDtypeStruct((lat_count, CINP, side_lanes), bf16),
+        ],
+        in_specs=[vmem, vmem],
+        out_specs=[vmem, vmem],
         scratch_shapes=[
-            pltpu.SemaphoreType.DMA((32,)),
-            pltpu.SemaphoreType.DMA((32,)),
+            pltpu.SemaphoreType.DMA((33,)),
+            pltpu.SemaphoreType.DMA((33,)),
             pltpu.SemaphoreType.DMA,
         ],
         compiler_params=pltpu.CompilerParams(
             vmem_limit_bytes=VMEM_LIMIT, collective_id=0, has_side_effects=True
         ),
-    )(packed)
+    )(packed, packed_side)
     if not with_lon:
         gathered = lax.all_gather(gathered, "lon", tiled=True)
-    meta = gathered[:, 77:80, ::EDGE].astype(f32)
-    all_place = (meta[:, 0, :] * 16.0 + meta[:, 1, :]).astype(jnp.int32)
-    cell_total = TS * jnp.sum(meta[:, 2, :])
-    count = lon_count * lat_count
-    sector = jnp.arange(count, dtype=jnp.int32)[:, None] // lat_count
-    row_all = all_place // TCOLS
-    col_all = sector * TCOLS + all_place % TCOLS
-    key_all = (row_all * (TCOLS * lon_count) + col_all).reshape(-1)
+
+    def described(blocks):
+        meta = blocks[:, 77:80, 0:tile_count].astype(f32)
+        return (meta[:, 0, :] * 16.0 + meta[:, 1, :]).astype(jnp.int32), jnp.sum(meta[:, 2, :])
+
+    def found(want, keys):
+        numbers = np.arange(keys.shape[0] * tile_count, dtype=np.int32)
+        codes = jnp.asarray(numbers // tile_count * 8 + numbers % tile_count)
+        hit = want[:, :, None] == keys.reshape(-1)[None, None, :]
+        return 7 + jnp.sum(jnp.where(hit, codes - 7, 0), axis=2)
+
     off = np.array(OFFSETS, np.int32)
-    my_row = places // TCOLS
-    my_col = lax.axis_index("lon") * TCOLS + places % TCOLS
-    want_row = my_row[:, None] + off[None, :, 0]
-    want_col = (my_col[:, None] + off[None, :, 1]) % (TCOLS * lon_count)
-    want = want_row * (TCOLS * lon_count) + want_col
-    hit = want[:, :, None] == key_all[None, None, :]
-    where = jnp.sum(jnp.where(hit, jnp.arange(count * tile_count, dtype=jnp.int32) + 1, 0), axis=2) - 1
-    near = jnp.stack(
-        [jnp.maximum(where, 0) // tile_count, jnp.where(where < 0, -1, where % tile_count)], axis=2
-    )
+    want_row = (places >> 3)[:, None] + off[None, :, 0]
+    want_col = (places & 7)[:, None] + off[None, :, 1]
+    all_place, ocean_rows = described(gathered)
+    if with_lon:
+        side_place, side_rows = described(sides)
+        cell_total = TS * (ocean_rows + side_rows)
+        inside = (want_col >= 0) & (want_col < TCOLS)
+        want = want_row * TCOLS + (want_col & 7)
+        near = jnp.concatenate(
+            [
+                found(jnp.where(inside, want, -1), all_place),
+                found(jnp.where(inside, -1, want), side_place),
+            ],
+            axis=1,
+        )
+    else:
+        cell_total = TS * ocean_rows
+        around = TCOLS * lon_count
+        sector = jnp.arange(lon_count * lat_count, dtype=jnp.int32)[:, None] // lat_count
+        keys = (all_place >> 3) * around + sector * TCOLS + (all_place & 7)
+        want_col = (want_col + lax.axis_index("lon") * TCOLS) % around
+        near = found(want_row * around + want_col, keys)
+    pick = halo_pick(with_lon)
     groups = lon_count * 4
     per = -(-USED // (groups * 4))
     tiles_all = per * groups * 4
     result, packed_sums = pl.pallas_call(
-        block_kernel,
+        functools.partial(block_kernel, with_lon),
         out_shape=[
             jax.ShapeDtypeStruct((tile_count, chan, CELLS), bf16),
             jax.ShapeDtypeStruct((tiles_all, 16, 128), bf16),
         ],
-        in_specs=[smem, smem] + [vmem] * 9,
+        in_specs=[smem, smem] + [vmem] * 10,
         out_specs=[vmem] * 2,
         scratch_shapes=[
             pltpu.VMEM((ROWT * 16, WIDE), f32),
             pltpu.VMEM((128, 256), f32),
-            pltpu.VMEM((tile_count, CINP, KROWS), bf16),
+            pltpu.VMEM((CINP, chan), bf16),
+            pltpu.VMEM((tile_count, CINP, pick.shape[0]), bf16),
             pltpu.VMEM((tile_count, CINP, PR * PC), f32),
             pltpu.VMEM((PR, PC, chan), f32),
             pltpu.VMEM((TS, TS, chan), f32),
@@ -433,8 +489,8 @@
         ],
         compiler_params=params,
     )(
-        near, rows, gathered, inputs, upstream, jnp.asarray(halo_pick(), bf16),
-        jnp.pad(stem_w, ((0, CINP - cin), (0, 0))), dw_kernel.T, norm_gain[None], w_in, w_out,
+        near, rows, gathered, sides, inputs, upstream, jnp.asarray(pick, bf16),
+        stem_w, dw_kernel.T, norm_gain[None], w_in, w_out.T,
     )
     span = per * 4
     reduced = pl.pallas_call(
@@ -457,8 +513,8 @@
         unpack_kernel,
         out_shape=[
             jax.ShapeDtypeStruct((chan, hid), f32),
-            jax.ShapeDtypeStruct((hid, chan), f32),
-            jax.ShapeDtypeStruct((chan, KW * KW), f32),
+            jax.ShapeDtypeStruct((chan, hid), f32),
+            jax.ShapeDtypeStruct((KW * KW, chan), f32),
             jax.ShapeDtypeStruct((1, chan), f32),
         ],
         in_specs=[smem, vmem],
@@ -466,7 +522,7 @@
         scratch_shapes=[pltpu.VMEM((ROWT * 16, WIDE), f32)],
         compiler_params=params,
     )(cell_total.reshape(1), reduced)
-    return result[None], sum_in, sum_out, sum_kernel, sum_gain[0]
+    return result[None], sum_in, sum_out.T, sum_kernel.T, sum_gain[0]
 
 
 def solution(mesh):

time: 115 us -> 115 us (level)
  local copies, waits for them, and re-layouts: 10 us -> 1.77 us
  Pallas kernels: 99.9 us -> 105 us
  other arithmetic: 2.43 us -> 5.24 us
    unnamed x6 -> x1, local copies, waits for them, and re-layouts: 6.44 us -> 1.6 us
    pallas_call x1, Pallas kernels: 31.6 us -> 35.3 us  [body(): pl.pallas_call(functools.partial(reduce_kernel, lon_count, per), out_shap...]
    convert_element_type x2 -> x3, other arithmetic: 0.08 us -> 1.61 us  [the longest x2 1.54 us: described(): meta = blocks[:, 77:80, 0:tile_count].astype(f32)]
    pad x1 -> x0, local copies, waits for them, and re-layouts: 1.41 us -> none  [body(): jnp.pad(stem_w, ((0, CINP - cin), (0, 0)))]
    pallas_call x3, Pallas kernels: 65.8 us -> 67.1 us  [the longest x1 37.4 us: body(): pl.pallas_call(functools.partial(block_kernel, with_lon), out_shape=[jax....]
    slice x1 -> x0, local copies, waits for them, and re-layouts: 1.19 us -> none  [body(): meta = gathered[:, 77:80, ::EDGE].astype(f32)]
where the time goes in v3:
time: 115 us; the launch traced here: 114 us
  Pallas kernels  105 us (91%)
  other arithmetic  5.24 us (5%)
  between operations  1.99 us (2%)
  local copies, waits for them, and re-layouts  1.77 us (2%)
    pallas_call x1, Pallas kernels, body(): pl.pallas_call(functools.partial(block_kernel, with_lon), out_shape=[jax....  37.4 us
    pallas_call x1, Pallas kernels, body(): pl.pallas_call(functools.partial(reduce_kernel, lon_count, per), out_shap...  35.3 us
    pallas_call x1, Pallas kernels, body(): pl.pallas_call(functools.partial(gather_kernel, with_lon), out_shape=[jax...  27.6 us
    pallas_call x1, Pallas kernels, body(): pl.pallas_call(unpack_kernel, out_shape=[jax.ShapeDtypeStruct((chan, hid)...  2.33 us

profile of v3, /device:TPU:0, one launch (start us, length us, event | category | flops | bytes accessed | tf_op | source)
XLA Modules:
  0.0 113.7 jit_solution(23152970900142015)
XLA Ops:
  0.6 0.7 broadcast_and_fusion
  1.3 0.7 fusion.6
  2.0 1.6 %copy.25 = bf16[1,4,77,256]{3,2,1,0:T(8,128)(2,1)} copy(bf16[1,4,77,256]{3,1,2,0:T(4,128)(2,1)} %param.16) | data formatting | bytes 315392 | tf_op args[0]
  3.6 2.1 %shard_map.191 = (bf16[80,640]{1,0:T(8,128)(2,1)}, bf16[80,256]{1,0:T(8,128)(2,1)}) custom-call(s32[4]{0:T(128)} %bitcast.24, s32[4]{0:T(128)} %bitcast.21, bf16[4,77,256]{2,1,0:T(8,128)(2,1)} %bitcast.16, bf16[256,160]{1,0:T(8,128)(2,1)} %constant.13.clone.pick_ref, bf16[2,256,64]{2,1,0:T(8,128)(2,1)} %constant.34.clone.side_ref), custom_call_target="tpu_custom_call" | custom-call | tf_op jit(solution)/shard_map/pallas_call | solution.py:396
  5.7 27.6 %shard_map.192 = (bf16[16,80,640]{2,1,0:T(8,128)(2,1)}, bf16[16,80,256]{2,1,0:T(8,128)(2,1)}) custom-call(bf16[80,640]{1,0:T(8,128)(2,1)} %get-tuple-element.15.src, bf16[80,256]{1,0:T(8,128)(2,1)} %get-tuple-element.16.side), custom_call_target="tpu_custom_call" | custom-call | tf_op jit(solution)/shard_map/pallas_call | solution.py:408
  33.3 0.8 slice_convert_fusion.1
  34.1 0.8 slice_convert_fusion
  34.9 0.6 slice_reduce_fusion
  36.8 0.1 fusion.1
  36.9 0.1 convert_element_type.31
  37.0 0.1 convert_element_type.28
  37.0 0.9 select_reduce_fusion.1
  38.0 0.7 pad_add_fusion.near
  38.7 37.4 %shard_map.193 = (bf16[4,200,256]{2,1,0:T(8,128)(2,1)}, bf16[192,16,128]{2,1,0:T(8,128)(2,1)}) custom-call(s32[4,16]{1,0:T(4,128)} %pad_add_fusion.near, s32[4]{0:T(128)} %bitcast.22, bf16[16,80,640]{2,1,0:T(8,128)(2,1)} %get-tuple-element.17.gathered, bf16[16,80,256]{2,1,0:T(8,128)(2,1)} %get-tuple-element.18.sides, bf16[4,77,256]{2,1,0:T(8,128)(2,1)} %bitcast.17, ...), custom_call_target="tpu_custom_call" | custom-call | tf_op jit(solution)/shard_map/pallas_call | solution.py:465
  76.0 35.3 %shard_map.194.tiles_ref = bf16[192,16,128]{2,1,0:T(8,128)(2,1)} custom-call(bf16[192,16,128]{2,1,0:T(8,128)(2,1)} %get-tuple-element.20.src), custom_call_target="tpu_custom_call" | custom-call | tf_op jit(solution)/shard_map/pallas_call | solution.py:496
  111.4 2.3 %shard_map.195 = (f32[200,800]{1,0:T(8,128)}, f32[200,800]{1,0:T(8,128)}, f32[49,200]{1,0:T(8,128)}, f32[1,200]{1,0:T(1,128)}) custom-call(f32[1]{0:T(128)} %bitcast.8.total_ref, bf16[192,16,128]{2,1,0:T(8,128)(2,1)} %shard_map.194.tiles_ref), custom_call_target="tpu_custom_call" | custom-call | tf_op jit(solution)/shard_map/pallas_call | solution.py:512
  (2 shorter events, 0.0 us)

commit v4 on v3

--- a/solution.py
+++ b/solution.py
@@ -18,34 +18,37 @@
 PC = 24
 CINP = 80
 SIDE_CELLS = 64
-KEDGE = CELLS + 8 * EDGE
+SLAB = 128
+REST = EDGE - SLAB
+KROWS = CELLS + 9 * SLAB
 OFFSETS = ((-1, -1), (-1, 0), (-1, 1), (0, -1), (0, 1), (1, -1), (1, 0), (1, 1))
 SIDE = 896
 WIDE = 2 * SIDE
 ROWT = 13
 USED = ROWT * WIDE // 128
-CROSS = tuple(n for n, (dy, dx) in enumerate(OFFSETS) if dx != 0)
 VMEM_LIMIT = 56 * 1024 * 1024
 
 
-def edge_index():
-    table = -np.ones((TS, TS), np.int64)
-    count = 0
-    for y in range(TS):
-        for x in range(TS):
-            if min(y, x) < REACH or max(y, x) >= TS - REACH:
-                table[y, x] = count
-                count += 1
-    return table
+def edge_lane(y, x):
+    low, high = REACH, TS - REACH
+    if x < low:
+        return y * REACH + x
+    if x >= high:
+        return SIDE_CELLS + y * REACH + x - high
+    if y < low:
+        middle = y * (high - low) + x - low
+        return 48 + middle if middle < 16 else 96 + middle
+    if y >= high:
+        return SLAB + (y - high) * (high - low) + x - low
+    return -1
 
 
 def edge_pick():
-    table = edge_index()
     pick = np.zeros((CELLS, EDGE), np.float32)
     for y in range(TS):
         for x in range(TS):
-            if table[y, x] >= 0:
-                pick[y * TS + x, table[y, x]] = 1
+            if edge_lane(y, x) >= 0:
+                pick[y * TS + x, edge_lane(y, x)] = 1
     return pick
 
 
@@ -58,9 +61,8 @@
     return pick
 
 
-def halo_pick(with_lon):
-    table = edge_index()
-    pick = np.zeros((KEDGE + 6 * SIDE_CELLS * with_lon, PR * PC), np.float32)
+def halo_pick(tile_count):
+    pick = np.zeros((KROWS, PR * PC), np.float32)
     for py in range(PR):
         for px in range(PR):
             y, x = py - REACH, px - REACH
@@ -68,12 +70,13 @@
             cell = py * PC + px
             if (dy, dx) == (0, 0):
                 pick[y * TS + x, cell] = 1
+                continue
+            lane = edge_lane(y % TS, x % TS)
+            if lane < SLAB:
+                pick[CELLS + OFFSETS.index((dy, dx)) * SLAB + lane, cell] = 1
             else:
-                n = OFFSETS.index((dy, dx))
-                pick[CELLS + n * EDGE + table[y % TS, x % TS], cell] = 1
-                if with_lon and dx != 0:
-                    part = (y % TS) * REACH + (x % TS if dx > 0 else x % TS - TS + REACH)
-                    pick[KEDGE + CROSS.index(n) * SIDE_CELLS + part, cell] = 1
+                for a in range(tile_count):
+                    pick[CELLS + 8 * SLAB + a * REST + lane - SLAB, cell] = 1
     return pick
 
 
@@ -85,9 +88,10 @@
     for a in range(tile_count):
         keep = (cell_row < rows[a]).astype(jnp.float32)
         tile = (x_ref[a].astype(jnp.float32) * keep).astype(jnp.bfloat16)
-        held[0:cin, a * EDGE : (a + 1) * EDGE] = jnp.dot(
-            tile, pick_ref[...], preferred_element_type=jnp.float32
-        )
+        edges = jnp.dot(tile, pick_ref[...], preferred_element_type=jnp.float32)
+        held[0:cin, a * SLAB : (a + 1) * SLAB] = edges[:, 0:SLAB]
+        base = tile_count * SLAB + a * REST
+        held[0:cin, base : base + REST] = edges[:, SLAB:EDGE]
         outer = jnp.where((places[a] & (TCOLS - 1)) == 0, side_ref[0], side_ref[1])
         held_side[0:cin, a * SIDE_CELLS : (a + 1) * SIDE_CELLS] = jnp.dot(
             tile, outer, preferred_element_type=jnp.float32
@@ -128,23 +132,27 @@
         keep = (lane_row < rows[a]).astype(f32)
         tile = (x_ref[a].astype(f32) * keep).astype(bf16)
         sources[a, 0:cin, 0:CELLS] = tile
-        for n in range(8):
+        for n, (dy, dx) in enumerate(OFFSETS):
             code = near[a, n]
             slot = code & 7
-            block = gathered[code >> 3]
-            piece = jnp.zeros((CINP, EDGE), bf16)
-            for j in range(tile_count):
-                piece = jnp.where(slot == j, block[:, j * EDGE : (j + 1) * EDGE], piece)
-            sources[a, :, CELLS + n * EDGE : CELLS + (n + 1) * EDGE] = piece
-        for m, n in enumerate(CROSS if with_lon else ()):
-            code = near[a, 8 + n]
-            slot = code & 7
-            block = sides[code >> 3]
-            piece = jnp.zeros((CINP, SIDE_CELLS), bf16)
-            for j in range(tile_count):
-                piece = jnp.where(slot == j, block[:, j * SIDE_CELLS : (j + 1) * SIDE_CELLS], piece)
-            start = KEDGE + m * SIDE_CELLS
-            sources[a, :, start : start + SIDE_CELLS] = piece
+            from_lane = pl.multiple_of((slot & 3) * SLAB, SLAB)
+            piece = gathered[code >> 3, :, pl.ds(from_lane, SLAB)]
+            piece = jnp.where(slot < tile_count, piece, jnp.zeros_like(piece))
+            if with_lon and dx != 0:
+                other = near[a, 8 + n]
+                spot = other & 7
+                from_lane = pl.multiple_of(((spot & 3) >> 1) * SLAB, SLAB)
+                outer = sides[other >> 3, :, pl.ds(from_lane, SLAB)]
+                turned = jnp.concatenate([outer[:, SIDE_CELLS:], outer[:, :SIDE_CELLS]], axis=1)
+                outer = jnp.where((spot & 1) == (0 if dx > 0 else 1), outer, turned)
+                piece = jnp.where(spot < tile_count, outer, piece)
+            sources[a, :, CELLS + n * SLAB : CELLS + (n + 1) * SLAB] = piece
+            if (dy, dx) == (-1, 0):
+                rest = gathered[code >> 3, :, tile_count * SLAB : tile_count * EDGE]
+                rest_of = lax.broadcasted_iota(jnp.int32, rest.shape, 1) // REST
+                sources[a, :, CELLS + 8 * SLAB :] = (
+                    rest.astype(f32) * (rest_of == slot).astype(f32)
+                ).astype(bf16)
     raw[...] = jnp.dot(
         sources[...].reshape(tile_count * CINP, pick_ref.shape[0]), pick_ref[...], preferred_element_type=f32
     ).reshape(tile_count, CINP, PR * PC)
@@ -319,22 +327,32 @@
     own.wait()
 
 
-def reduce_kernel(n_lon, per, src, out, first, acc, second, third, sems):
+def reduce_kernel(n_lon, per, src, out, first, middle, second, acc, fourth, third, sems):
     lat, lon = lax.axis_index("lat"), lax.axis_index("lon")
-    z = lat // 4
-    groups, deep = n_lon * 4, 4
+    z, x, core = lat // 4, (lat // 2) % 2, lat % 2
+    chips, deep = n_lon * 2, 4
     span = per * deep
-    mine = lon * 4 + lat % 4
-
-    def in_plane(d):
-        g = (mine + d) % groups
-        return g, {"lat": z * 4 + g % 4, "lon": g // 4}
+
+    def chip(d):
+        return (lon * 2 + x + d) % chips
+
+    def device_at(d):
+        q = chip(d)
+        return {"lat": z * 4 + (q % 2) * 2 + core, "lon": q // 2}
 
     def along(d):
         other = (z + d) % deep
         return other, {"lat": other * 4 + lat % 4, "lon": lon}
 
-    greet([in_plane(d)[1] for d in range(1, groups)] + [along(d)[1] for d in range(1, deep)])
+    def region(d, half):
+        return pl.ds((chip(d) * 2 + half) * span, span)
+
+    partner = {"lat": z * 4 + x * 2 + 1 - core, "lon": lon}
+    greet(
+        [partner]
+        + [device_at(d) for d in range(1, chips)]
+        + [along(d)[1] for d in range(1, deep)]
+    )
     copies = []
 
     def send(stage, back, here, there, device):
@@ -346,35 +364,49 @@
         copies.append(copy)
         return copy
 
+    f32, bf16 = jnp.float32, jnp.bfloat16
+    order = list(range(1, chips)) + [0]
+    halves = {}
+    for d in order:
+        halves[d] = send(0, d, src.at[region(d, 1 - core)], first.at[d], partner)
     landing = []
-    for d in range(1, groups):
-        g, device = in_plane(d)
-        landing.append(send(0, groups - d, src.at[pl.ds(g * span, span)], first.at[groups - d], device))
-    acc[...] = src[pl.ds(mine * span, span)].astype(jnp.float32)
-    for d in range(1, groups):
+    for d in order:
+        halves[d].wait_recv()
+        pair = src[region(d, core)].astype(f32) + first[d].astype(f32)
+        if d == 0:
+            acc[...] = pair
+        else:
+            middle[d] = pair.astype(bf16)
+            landing.append(send(1, chips - d, middle.at[d], second.at[chips - d], device_at(d)))
+    for d in range(1, chips):
         landing[d - 1].wait_recv()
-        acc[...] += first[groups - d].astype(jnp.float32)
-    second[...] = acc[...].astype(jnp.bfloat16)
+        acc[...] += second[chips - d].astype(f32)
+    fourth[...] = acc[...].astype(bf16)
     landing = []
     for d in range(1, deep):
         other, device = along(d)
-        landing.append(send(1, deep - d, second.at[pl.ds(other * per, per)], third.at[deep - d], device))
+        landing.append(send(2, deep - d, fourth.at[pl.ds(other * per, per)], third.at[deep - d], device))
     total = acc[pl.ds(z * per, per)]
     for d in range(1, deep):
         landing[d - 1].wait_recv()
-        total += third[deep - d].astype(jnp.float32)
-    mark = pl.ds(mine * span + z * per, per)
-    out[mark] = total.astype(jnp.bfloat16)
+        total += third[deep - d].astype(f32)
+    mark = pl.ds((chip(0) * 2 + core) * span + z * per, per)
+    out[mark] = total.astype(bf16)
     landing = []
     for d in range(1, deep):
-        landing.append(send(2, deep - d, out.at[mark], out.at[mark], along(d)[1]))
+        landing.append(send(3, deep - d, out.at[mark], out.at[mark], along(d)[1]))
     for copy in landing:
         copy.wait_recv()
-    whole = pl.ds(mine * span, span)
+    whole = region(0, core)
     landing = []
-    for d in range(1, groups):
-        landing.append(send(3, groups - d, out.at[whole], out.at[whole], in_plane(d)[1]))
-    for copy in landing:
+    for d in range(1, chips):
+        landing.append(send(4, chips - d, out.at[whole], out.at[whole], device_at(d)))
+    final = [send(5, 0, out.at[whole], out.at[whole], partner)]
+    for d in range(1, chips):
+        landing[d - 1].wait_recv()
+        came = region(chips - d, core)
+        final.append(send(5, chips - d, out.at[came], out.at[came], partner))
+    for copy in final:
         copy.wait_recv()
     for copy in copies:
         copy.wait_send()
@@ -458,7 +490,7 @@
         keys = (all_place >> 3) * around + sector * TCOLS + (all_place & 7)
         want_col = (want_col + lax.axis_index("lon") * TCOLS) % around
         near = found(want_row * around + want_col, keys)
-    pick = halo_pick(with_lon)
+    pick = halo_pick(tile_count)
     groups = lon_count * 4
     per = -(-USED // (groups * 4))
     tiles_all = per * groups * 4
@@ -493,17 +525,20 @@
         stem_w, dw_kernel.T, norm_gain[None], w_in, w_out.T,
     )
     span = per * 4
+    chips = lon_count * 2
     reduced = pl.pallas_call(
         functools.partial(reduce_kernel, lon_count, per),
         out_shape=jax.ShapeDtypeStruct((tiles_all, 16, 128), bf16),
         in_specs=[vmem],
         out_specs=vmem,
         scratch_shapes=[
-            pltpu.VMEM((groups, span, 16, 128), bf16),
+            pltpu.VMEM((chips, span, 16, 128), bf16),
+            pltpu.VMEM((chips, span, 16, 128), bf16),
+            pltpu.VMEM((chips, span, 16, 128), bf16),
             pltpu.VMEM((span, 16, 128), f32),
             pltpu.VMEM((span, 16, 128), bf16),
             pltpu.VMEM((4, per, 16, 128), bf16),
-            pltpu.SemaphoreType.DMA((4, 2, groups)),
+            pltpu.SemaphoreType.DMA((6, 2, max(chips, 4))),
         ],
         compiler_params=pltpu.CompilerParams(
             vmem_limit_bytes=VMEM_LIMIT, collective_id=1, has_side_effects=True

time: 115 us -> 103 us (0.90)
  Pallas kernels: 105 us -> 93.4 us
    pallas_call x1, Pallas kernels: 37.4 us -> 30.1 us  [body(): pl.pallas_call(functools.partial(block_kernel, with_lon), out_shape=[jax....]
    pallas_call x1, Pallas kernels: 35.3 us -> 31.3 us  [body(): pl.pallas_call(functools.partial(reduce_kernel, lon_count, per), out_shap...]
where the time goes in v4:
time: 103 us; the launch traced here: 102 us
  Pallas kernels  93.4 us (91%)
  other arithmetic  5.24 us (5%)
  between operations  1.99 us (2%)
  local copies, waits for them, and re-layouts  1.77 us (2%)
    pallas_call x1, Pallas kernels, body(): pl.pallas_call(functools.partial(reduce_kernel, lon_count, per), out_shap...  31.3 us
    pallas_call x1, Pallas kernels, body(): pl.pallas_call(functools.partial(block_kernel, with_lon), out_shape=[jax....  30.1 us
    pallas_call x1, Pallas kernels, body(): pl.pallas_call(functools.partial(gather_kernel, with_lon), out_shape=[jax...  27.6 us
    pallas_call x1, Pallas kernels, body(): pl.pallas_call(unpack_kernel, out_shape=[jax.ShapeDtypeStruct((chan, hid)...  2.33 us

profile of v4, /device:TPU:0, one launch (start us, length us, event | category | flops | bytes accessed | tf_op | source)
XLA Modules:
  0.0 102.4 jit_solution(950894953511963822)
XLA Ops:
  0.6 0.7 broadcast_and_fusion
  1.3 0.7 fusion.6
  2.0 1.6 %copy.25 = bf16[1,4,77,256]{3,2,1,0:T(8,128)(2,1)} copy(bf16[1,4,77,256]{3,1,2,0:T(4,128)(2,1)} %param.16) | data formatting | bytes 315392 | tf_op args[0]
  3.6 2.0 %shard_map.191 = (bf16[80,640]{1,0:T(8,128)(2,1)}, bf16[80,256]{1,0:T(8,128)(2,1)}) custom-call(s32[4]{0:T(128)} %bitcast.24, s32[4]{0:T(128)} %bitcast.21, bf16[4,77,256]{2,1,0:T(8,128)(2,1)} %bitcast.16, bf16[256,160]{1,0:T(8,128)(2,1)} %constant.13.clone.pick_ref, bf16[2,256,64]{2,1,0:T(8,128)(2,1)} %constant.34.clone.side_ref), custom_call_target="tpu_custom_call" | custom-call | tf_op jit(solution)/shard_map/pallas_call | solution.py:428
  5.7 27.6 %shard_map.192 = (bf16[16,80,640]{2,1,0:T(8,128)(2,1)}, bf16[16,80,256]{2,1,0:T(8,128)(2,1)}) custom-call(bf16[80,640]{1,0:T(8,128)(2,1)} %get-tuple-element.15.src, bf16[80,256]{1,0:T(8,128)(2,1)} %get-tuple-element.16.side), custom_call_target="tpu_custom_call" | custom-call | tf_op jit(solution)/shard_map/pallas_call | solution.py:440
  33.3 0.8 slice_convert_fusion.1
  34.1 0.8 slice_convert_fusion
  34.8 0.6 slice_reduce_fusion
  36.8 0.1 fusion.1
  36.8 0.1 convert_element_type.31
  36.9 0.1 convert_element_type.28
  37.0 0.9 select_reduce_fusion.1
  38.0 0.7 pad_add_fusion.near
  38.6 30.1 %shard_map.193 = (bf16[4,200,256]{2,1,0:T(8,128)(2,1)}, bf16[192,16,128]{2,1,0:T(8,128)(2,1)}) custom-call(s32[4,16]{1,0:T(4,128)} %pad_add_fusion.near, s32[4]{0:T(128)} %bitcast.22, bf16[16,80,640]{2,1,0:T(8,128)(2,1)} %get-tuple-element.17.gathered, bf16[16,80,256]{2,1,0:T(8,128)(2,1)} %get-tuple-element.18.sides, bf16[4,77,256]{2,1,0:T(8,128)(2,1)} %bitcast.17, ...), custom_call_target="tpu_custom_call" | custom-call | tf_op jit(solution)/shard_map/pallas_call | solution.py:497
  68.8 31.3 %shard_map.194.tiles_ref = bf16[192,16,128]{2,1,0:T(8,128)(2,1)} custom-call(bf16[192,16,128]{2,1,0:T(8,128)(2,1)} %get-tuple-element.20.src), custom_call_target="tpu_custom_call" | custom-call | tf_op jit(solution)/shard_map/pallas_call | solution.py:529
  100.1 2.3 %shard_map.195 = (f32[200,800]{1,0:T(8,128)}, f32[200,800]{1,0:T(8,128)}, f32[49,200]{1,0:T(8,128)}, f32[1,200]{1,0:T(1,128)}) custom-call(f32[1]{0:T(128)} %bitcast.8.total_ref, bf16[192,16,128]{2,1,0:T(8,128)(2,1)} %shard_map.194.tiles_ref), custom_call_target="tpu_custom_call" | custom-call | tf_op jit(solution)/shard_map/pallas_call | solution.py:547
  (2 shorter events, 0.0 us)

commit v5 on v4

--- a/solution.py
+++ b/solution.py
@@ -163,19 +163,22 @@
         stems = jnp.dot(cells_in, stem_s[...], preferred_element_type=f32)
         padded[...] = stems.astype(bf16).astype(f32).reshape(PR, PC, chan)
 
-        @pl.loop(0, TS // 4)
+        @pl.loop(0, TS // 8)
         def _(yb):
-            y0 = yb * 4
-            acc = jnp.zeros((4, TS, chan), f32)
-            for k in range(KW):
-                shifted = padded[pl.ds(y0, 4 + KW - 1), k : k + TS, :]
-                for r in range(KW):
-                    acc += taps_ref[r * KW + k : r * KW + k + 1, :][None] * shifted[r : r + 4]
+            y0 = yb * 8
+            for lo, hi in ((0, 128), (128, chan)):
+                acc = jnp.zeros((8, TS, hi - lo), f32)
+                for k in range(KW):
+                    shifted = padded[pl.ds(y0, 8 + KW - 1), k : k + TS, lo:hi]
+                    for r in range(KW):
+                        acc += taps_ref[r * KW + k : r * KW + k + 1, lo:hi][None] * shifted[r : r + 8]
+                unit_s[pl.ds(y0, 8), :, lo:hi] = acc
+            acc = unit_s[pl.ds(y0, 8)]
             mean = jnp.mean(acc, axis=2, keepdims=True)
             centred = acc - mean
             inv = lax.rsqrt(jnp.mean(centred * centred, axis=2, keepdims=True) + 1e-06)
-            unit_s[pl.ds(y0, 4)] = centred * inv
-            inv_s[pl.ds(y0, 4)] = jnp.broadcast_to(inv, (4, TS, 128))
+            unit_s[pl.ds(y0, 8)] = centred * inv
+            inv_s[pl.ds(y0, 8)] = jnp.broadcast_to(inv, (8, TS, 128))
 
         gain = gain_ref[...]
         unit = unit_s[...].reshape(CELLS, chan)
@@ -209,15 +212,16 @@
         inv = inv_s[...].reshape(CELLS, 128)[:, 0:1]
         gconv[...] = (inv * (scaled - first - unit * second)).reshape(TS, TS, chan)
 
-        @pl.loop(0, TS // 4)
+        @pl.loop(0, TS // 8)
         def _(yb):
-            y0 = yb * 4
-            grad = gconv[pl.ds(y0, 4)]
-            for k in range(KW):
-                shifted = padded[pl.ds(y0, 4 + KW - 1), k : k + TS, :]
-                for r in range(KW):
-                    prod = grad * shifted[r : r + 4]
-                    kacc[r * KW + k] += jnp.sum(prod.reshape(8, 8, chan), axis=0)
+            y0 = yb * 8
+            for lo, hi in ((0, 128), (128, chan)):
+                grad = gconv[pl.ds(y0, 8), :, lo:hi]
+                for k in range(KW):
+                    shifted = padded[pl.ds(y0, 8 + KW - 1), k : k + TS, lo:hi]
+                    for r in range(KW):
+                        prod = grad * shifted[r : r + 8]
+                        kacc[r * KW + k, :, lo:hi] += jnp.sum(prod.reshape(16, 8, hi - lo), axis=0)
 
     held[...] = jnp.zeros_like(held)
     small[...] = jnp.zeros_like(small)

time: 103 us -> 102 us (level)
  no operation moved by 1% of the time
where the time goes in v5:
time: 102 us
  Pallas kernels  92.6 us (91%)
  other arithmetic  5.24 us (5%)
  between operations  1.99 us (2%)
  local copies, waits for them, and re-layouts  1.77 us (2%)
    pallas_call x1, Pallas kernels, body(): pl.pallas_call(functools.partial(reduce_kernel, lon_count, per), out_shap...  31.3 us
    pallas_call x1, Pallas kernels, body(): pl.pallas_call(functools.partial(block_kernel, with_lon), out_shape=[jax....  29.4 us
    pallas_call x1, Pallas kernels, body(): pl.pallas_call(functools.partial(gather_kernel, with_lon), out_shape=[jax...  27.6 us
    pallas_call x1, Pallas kernels, body(): pl.pallas_call(unpack_kernel, out_shape=[jax.ShapeDtypeStruct((chan, hid)...  2.33 us
    pallas_call x1, Pallas kernels, body(): pl.pallas_call(pack_kernel, out_shape=[jax.ShapeDtypeStruct((CINP, lanes)...  2.04 us

profile of v5, /device:TPU:0, one launch (start us, length us, event | category | flops | bytes accessed | tf_op | source)
XLA Modules:
  0.0 101.6 jit_solution(11123718891252376215)
XLA Ops:
  0.6 0.7 broadcast_and_fusion
  1.3 0.7 fusion.6
  2.0 1.6 %copy.25 = bf16[1,4,77,256]{3,2,1,0:T(8,128)(2,1)} copy(bf16[1,4,77,256]{3,1,2,0:T(4,128)(2,1)} %param.16) | data formatting | bytes 315392 | tf_op args[0]
  3.6 2.0 %shard_map.191 = (bf16[80,640]{1,0:T(8,128)(2,1)}, bf16[80,256]{1,0:T(8,128)(2,1)}) custom-call(s32[4]{0:T(128)} %bitcast.24, s32[4]{0:T(128)} %bitcast.21, bf16[4,77,256]{2,1,0:T(8,128)(2,1)} %bitcast.16, bf16[256,160]{1,0:T(8,128)(2,1)} %constant.13.clone.pick_ref, bf16[2,256,64]{2,1,0:T(8,128)(2,1)} %constant.34.clone.side_ref), custom_call_target="tpu_custom_call" | custom-call | tf_op jit(solution)/shard_map/pallas_call | solution.py:432
  5.7 27.6 %shard_map.192 = (bf16[16,80,640]{2,1,0:T(8,128)(2,1)}, bf16[16,80,256]{2,1,0:T(8,128)(2,1)}) custom-call(bf16[80,640]{1,0:T(8,128)(2,1)} %get-tuple-element.15.src, bf16[80,256]{1,0:T(8,128)(2,1)} %get-tuple-element.16.side), custom_call_target="tpu_custom_call" | custom-call | tf_op jit(solution)/shard_map/pallas_call | solution.py:444
  33.3 0.8 slice_convert_fusion.1
  34.1 0.8 slice_convert_fusion
  34.8 0.6 slice_reduce_fusion
  36.8 0.1 fusion.1
  36.8 0.1 convert_element_type.31
  36.9 0.1 convert_element_type.28
  37.0 0.9 select_reduce_fusion.1
  38.0 0.7 pad_add_fusion.near
  38.6 29.4 %shard_map.193 = (bf16[4,200,256]{2,1,0:T(8,128)(2,1)}, bf16[192,16,128]{2,1,0:T(8,128)(2,1)}) custom-call(s32[4,16]{1,0:T(4,128)} %pad_add_fusion.near, s32[4]{0:T(128)} %bitcast.22, bf16[16,80,640]{2,1,0:T(8,128)(2,1)} %get-tuple-element.17.gathered, bf16[16,80,256]{2,1,0:T(8,128)(2,1)} %get-tuple-element.18.sides, bf16[4,77,256]{2,1,0:T(8,128)(2,1)} %bitcast.17, ...), custom_call_target="tpu_custom_call" | custom-call | tf_op jit(solution)/shard_map/pallas_call | solution.py:501
  68.0 31.3 %shard_map.194.tiles_ref = bf16[192,16,128]{2,1,0:T(8,128)(2,1)} custom-call(bf16[192,16,128]{2,1,0:T(8,128)(2,1)} %get-tuple-element.20.src), custom_call_target="tpu_custom_call" | custom-call | tf_op jit(solution)/shard_map/pallas_call | solution.py:533
  99.3 2.3 %shard_map.195 = (f32[200,800]{1,0:T(8,128)}, f32[200,800]{1,0:T(8,128)}, f32[49,200]{1,0:T(8,128)}, f32[1,200]{1,0:T(1,128)}) custom-call(f32[1]{0:T(128)} %bitcast.8.total_ref, bf16[192,16,128]{2,1,0:T(8,128)(2,1)} %shard_map.194.tiles_ref), custom_call_target="tpu_custom_call" | custom-call | tf_op jit(solution)/shard_map/pallas_call | solution.py:551
  (2 shorter events, 0.0 us)
